TPU v7x, 32 devices: a whole 2x2x4 slice. The times are simulated.
32 devices in a mesh: rep: 16 (over z, y, core), shard: 2 (over x).
Axes of the slice: x: 2, y: 2, z: 4, core: 2. Of those that a mesh axis runs over, the one named last changes fastest.
Arguments:
- tokens: bfloat16 [4096, 576], P(('rep', 'shard')), may hold values from -6 to 6
- block_order: int32 [16, 2], P('rep'), may hold values from 0 to 1, each once within a row
- attn_gain: bfloat16 [1, 576], P(None, 'shard'), may hold values from 0.5 to 1.5
- q_weight: bfloat16 [1, 576, 576], P(None, 'shard'), may hold values from -0.25 to 0.25
- k_weight: bfloat16 [1, 576, 192], P(None, 'shard'), may hold values from -0.25 to 0.25
- v_weight: bfloat16 [1, 576, 192], P(None, 'shard'), may hold values from -0.25 to 0.25
- o_weight: bfloat16 [1, 576, 576], P(None, 'shard'), may hold values from -3 to 3
- ffn_gain: bfloat16 [1, 576], P(None, 'shard'), may hold values from 0.5 to 1.5
- gate_weight: bfloat16 [1, 576, 1536], P(None, 'shard'), may hold values from -0.25 to 0.25
- up_weight: bfloat16 [1, 576, 1536], P(None, 'shard'), may hold values from -0.25 to 0.25
- down_weight: bfloat16 [1, 1536, 576], P(None, 'shard'), may hold values from -0.15625 to 0.15625
- cotangent: bfloat16 [4096, 576], P(('rep', 'shard')), may hold values from -6 to 6
Outputs:
- block_out: float32 [4096, 576], P(('rep', 'shard'))
- input_grad: float32 [4096, 576], P(('rep', 'shard'))
- grad_attn_gain: float32 [1, 576], P(None, 'shard')
- grad_q_weight: float32 [1, 576, 576], P(None, 'shard')
- grad_k_weight: float32 [1, 576, 192], P(None, 'shard')
- grad_v_weight: float32 [1, 576, 192], P(None, 'shard')
- grad_o_weight: float32 [1, 576, 576], P(None, 'shard')
- grad_ffn_gain: float32 [1, 576], P(None, 'shard')
- grad_gate_weight: float32 [1, 576, 1536], P(None, 'shard')
- grad_up_weight: float32 [1, 576, 1536], P(None, 'shard')
- grad_down_weight: float32 [1, 1536, 576], P(None, 'shard')
Inputs may be any that keep to these rules, and one draw needn't show every extreme that they name: `block_order`: each row lists every number 0 to 1 once.
All inputs are finite; a program needn't handle non-finite values.
Results may differ from a plain program's by a relative error of at most 0.012.
Values may be sent and summed in bfloat16 or wider, within the bound.
A program may use at most 128 MiB of HBM per device.

v0:
```python
import math

import jax
import jax.numpy as jnp
from jax import lax
from jax.sharding import PartitionSpec as P

H = 9
KV = 3
HD = 64
LAYERS = 1


rope_base = 100000.0
norm_eps = 1e-05


def rope_tables(positions, head_dim):
    half_dim = head_dim // 2
    frequency = jnp.exp(
        jnp.arange(half_dim, dtype=jnp.float32) * (-2.0 * math.log(rope_base) / head_dim)
    )
    angles = positions.astype(jnp.float32)[:, None] * frequency[None, :]
    return (jnp.cos(angles)[:, None, :], jnp.sin(angles)[:, None, :])


def rotate(tensor, cos_table, sin_table):
    half_dim = tensor.shape[-1] // 2
    first_half = tensor[..., :half_dim]
    second_half = tensor[..., half_dim:]
    return jnp.concatenate(
        [
            first_half * cos_table - second_half * sin_table,
            second_half * cos_table + first_half * sin_table,
        ],
        axis=-1,
    )


def rotate_back(tensor, cos_table, sin_table):
    half_dim = tensor.shape[-1] // 2
    first_half = tensor[..., :half_dim]
    second_half = tensor[..., half_dim:]
    return jnp.concatenate(
        [
            first_half * cos_table + second_half * sin_table,
            second_half * cos_table - first_half * sin_table,
        ],
        axis=-1,
    )


def rms_scale(hidden):
    factor = lax.rsqrt(jnp.mean(hidden * hidden, axis=-1, keepdims=True) + norm_eps)
    return (hidden * factor, factor)


def rms_back(grad_in, normed, factor, gain_row):
    scaled = grad_in * gain_row.astype(jnp.float32)
    return factor * (scaled - normed * jnp.mean(scaled * normed, axis=-1, keepdims=True))


def transposed_product(left, right):
    return jnp.einsum("tk,tn->kn", left, right, preferred_element_type=jnp.float32)


def gather_forward(params, layer_index):
    return (
        lax.all_gather(params[0][layer_index], "shard", axis=0, tiled=True),
        lax.all_gather(params[1][layer_index], "shard", axis=0, tiled=True),
        lax.all_gather(params[2][layer_index], "shard", axis=0, tiled=True),
        lax.all_gather(params[3][layer_index], "shard", axis=0, tiled=True),
        lax.all_gather(params[4][layer_index], "shard", axis=0, tiled=True),
        lax.all_gather(params[5][layer_index], "shard", axis=0, tiled=True),
        lax.all_gather(params[6][layer_index], "shard", axis=0, tiled=True),
        lax.all_gather(params[7][layer_index], "shard", axis=0, tiled=True),
        lax.all_gather(params[8][layer_index], "shard", axis=0, tiled=True),
    )


def gather_backward(params, layer_index):
    return (
        lax.all_gather(params[0][layer_index], "shard", axis=0, tiled=True),
        lax.all_gather(params[1][layer_index], "shard", axis=0, tiled=True),
        lax.all_gather(params[2][layer_index], "shard", axis=0, tiled=True),
        lax.all_gather(params[3][layer_index], "shard", axis=0, tiled=True),
        lax.all_gather(params[4][layer_index], "shard", axis=0, tiled=True),
        lax.all_gather(params[5][layer_index], "shard", axis=0, tiled=True),
        lax.all_gather(params[6][layer_index], "shard", axis=0, tiled=True),
        lax.all_gather(params[7][layer_index], "shard", axis=0, tiled=True),
        lax.all_gather(params[8][layer_index], "shard", axis=0, tiled=True),
    )


def visible_scores(query_grouped, all_keys, q_positions, key_positions):
    scores = jnp.einsum(
        "sgmd,tgd->gmst", query_grouped, all_keys, preferred_element_type=jnp.float32
    ) * HD ** (-0.5)
    allowed = key_positions[None, :] <= q_positions[:, None]
    return (jnp.where(allowed, scores, -1e30), allowed)


def layer_forward(hidden, gathered, q_positions, key_positions, cos_table, sin_table):
    attn_g, q_w, k_w, v_w, o_w, ffn_g, gate_w, up_w, down_w = gathered
    row_count = hidden.shape[0]
    head_groups = H // KV
    normed, factor = rms_scale(hidden)
    attn_in = (normed * attn_g.astype(jnp.float32)).astype(jnp.bfloat16)
    query_rows = rotate(
        jnp.dot(attn_in, q_w, preferred_element_type=jnp.float32).reshape(row_count, H, HD),
        cos_table,
        sin_table,
    ).astype(jnp.bfloat16)
    key_rows = rotate(
        jnp.dot(attn_in, k_w, preferred_element_type=jnp.float32).reshape(row_count, KV, HD),
        cos_table,
        sin_table,
    ).astype(jnp.bfloat16)
    value_rows = jnp.dot(attn_in, v_w, preferred_element_type=jnp.float32).astype(jnp.bfloat16)
    all_keys, all_values = (
        lax.all_gather(key_rows.reshape(row_count, KV * HD), "shard", axis=0, tiled=True),
        lax.all_gather(value_rows, "shard", axis=0, tiled=True),
    )
    all_keys = all_keys.reshape(-1, KV, HD)
    all_values = all_values.reshape(-1, KV, HD)
    query_grouped = query_rows.reshape(row_count, KV, head_groups, HD)
    scores, allowed = visible_scores(query_grouped, all_keys, q_positions, key_positions)
    row_max = jnp.max(scores, axis=-1, keepdims=True)
    row_total = jnp.sum(jnp.exp(scores - row_max), axis=-1, keepdims=True)
    log_total = (row_max + jnp.log(row_total))[..., 0]
    probs_bf = jnp.where(allowed, jnp.exp(scores - log_total[..., None]), 0.0).astype(jnp.bfloat16)
    attended = (
        jnp.einsum("gmst,tgd->sgmd", probs_bf, all_values, preferred_element_type=jnp.float32)
        .astype(jnp.bfloat16)
        .reshape(row_count, H * HD)
    )
    middle = hidden + jnp.dot(attended, o_w, preferred_element_type=jnp.float32)
    normed_two, factor_two = rms_scale(middle)
    ffn_in = (normed_two * ffn_g.astype(jnp.float32)).astype(jnp.bfloat16)
    gate_pre = jnp.dot(ffn_in, gate_w, preferred_element_type=jnp.float32)
    up_pre = jnp.dot(ffn_in, up_w, preferred_element_type=jnp.float32)
    mixed = (jax.nn.silu(gate_pre) * up_pre).astype(jnp.bfloat16)
    output = middle + jnp.dot(mixed, down_w, preferred_element_type=jnp.float32)
    saved = (
        normed,
        factor,
        attn_in,
        query_grouped,
        all_keys,
        all_values,
        log_total,
        attended,
        normed_two,
        factor_two,
        ffn_in,
        gate_pre,
        up_pre,
        mixed,
    )
    return (output, saved)


def layer_backward(gradient, saved, gathered, q_positions, key_positions, cos_table, sin_table):
    attn_g, q_w, k_w, v_w, o_w, ffn_g, gate_w, up_w, down_w = gathered
    (
        normed,
        factor,
        attn_in,
        query_grouped,
        all_keys,
        all_values,
        log_total,
        attended,
        normed_two,
        factor_two,
        ffn_in,
        gate_pre,
        up_pre,
        mixed,
    ) = saved
    row_count = gradient.shape[0]
    head_groups = H // KV
    grad_bf = gradient.astype(jnp.bfloat16)
    g_down = transposed_product(mixed, grad_bf)
    g_mixed = jnp.einsum("tn,kn->tk", grad_bf, down_w, preferred_element_type=jnp.float32)
    sigmoid_gate = jax.nn.sigmoid(gate_pre)
    g_up = (g_mixed * gate_pre * sigmoid_gate).astype(jnp.bfloat16)
    g_gate = (g_mixed * up_pre * sigmoid_gate * (1.0 + gate_pre * (1.0 - sigmoid_gate))).astype(
        jnp.bfloat16
    )
    g_gate_w = transposed_product(ffn_in, g_gate)
    g_up_w = transposed_product(ffn_in, g_up)
    g_ffn_in = jnp.einsum(
        "tn,kn->tk", g_gate, gate_w, preferred_element_type=jnp.float32
    ) + jnp.einsum("tn,kn->tk", g_up, up_w, preferred_element_type=jnp.float32)
    g_ffn_gain = jnp.sum(g_ffn_in * normed_two, axis=0)
    g_middle = gradient + rms_back(g_ffn_in, normed_two, factor_two, ffn_g)
    middle_bf = g_middle.astype(jnp.bfloat16)
    g_o_w = transposed_product(attended, middle_bf)
    g_attended = (
        jnp.einsum("tn,kn->tk", middle_bf, o_w, preferred_element_type=jnp.float32)
        .astype(jnp.bfloat16)
        .reshape(row_count, KV, head_groups, HD)
    )
    scores, allowed = visible_scores(query_grouped, all_keys, q_positions, key_positions)
    probs = jnp.where(allowed, jnp.exp(scores - log_total[..., None]), 0.0)
    probs_bf = probs.astype(jnp.bfloat16)
    value_terms = jnp.einsum(
        "gmst,sgmd->tgd", probs_bf, g_attended, preferred_element_type=jnp.float32
    )
    g_probs = jnp.einsum(
        "sgmd,tgd->gmst", g_attended, all_values, preferred_element_type=jnp.float32
    )
    delta = jnp.einsum(
        "sgmd,sgmd->gms",
        g_attended,
        attended.reshape(row_count, KV, head_groups, HD),
        preferred_element_type=jnp.float32,
    )
    g_scores = (probs * (g_probs - delta[..., None]) * HD ** (-0.5)).astype(jnp.bfloat16)
    g_query = jnp.einsum("gmst,tgd->sgmd", g_scores, all_keys, preferred_element_type=jnp.float32)
    key_terms = jnp.einsum(
        "gmst,sgmd->tgd", g_scores, query_grouped, preferred_element_type=jnp.float32
    )
    seq_rows = key_terms.shape[0]
    key_sum, value_sum = (
        lax.psum_scatter(
            key_terms.reshape(seq_rows, KV * HD), "shard", scatter_dimension=0, tiled=True
        ),
        lax.psum_scatter(
            value_terms.reshape(seq_rows, KV * HD), "shard", scatter_dimension=0, tiled=True
        ),
    )
    g_query_bf = (
        rotate_back(g_query.reshape(row_count, H, HD), cos_table, sin_table)
        .reshape(row_count, H * HD)
        .astype(jnp.bfloat16)
    )
    g_key_bf = (
        rotate_back(key_sum.reshape(row_count, KV, HD), cos_table, sin_table)
        .reshape(row_count, KV * HD)
        .astype(jnp.bfloat16)
    )
    g_value_bf = value_sum.astype(jnp.bfloat16)
    g_q_w = transposed_product(attn_in, g_query_bf)
    g_k_w = transposed_product(attn_in, g_key_bf)
    g_v_w = transposed_product(attn_in, g_value_bf)
    g_attn_in = (
        jnp.einsum("tn,kn->tk", g_query_bf, q_w, preferred_element_type=jnp.float32)
        + jnp.einsum("tn,kn->tk", g_key_bf, k_w, preferred_element_type=jnp.float32)
        + jnp.einsum("tn,kn->tk", g_value_bf, v_w, preferred_element_type=jnp.float32)
    )
    g_attn_gain = jnp.sum(g_attn_in * normed, axis=0)
    g_hidden = g_middle + rms_back(g_attn_in, normed, factor, attn_g)
    terms = (g_attn_gain, g_q_w, g_k_w, g_v_w, g_o_w, g_ffn_gain, g_gate_w, g_up_w, g_down)
    return (g_hidden, terms)


def share_terms(terms):
    return (
        lax.psum_scatter(terms[0], "shard", scatter_dimension=0, tiled=True),
        lax.psum_scatter(terms[1], "shard", scatter_dimension=0, tiled=True),
        lax.psum_scatter(terms[2], "shard", scatter_dimension=0, tiled=True),
        lax.psum_scatter(terms[3], "shard", scatter_dimension=0, tiled=True),
        lax.psum_scatter(terms[4], "shard", scatter_dimension=0, tiled=True),
        lax.psum_scatter(terms[5], "shard", scatter_dimension=0, tiled=True),
        lax.psum_scatter(terms[6], "shard", scatter_dimension=0, tiled=True),
        lax.psum_scatter(terms[7], "shard", scatter_dimension=0, tiled=True),
        lax.psum_scatter(terms[8], "shard", scatter_dimension=0, tiled=True),
    )


def replica_sum(shares):
    return lax.psum(
        (
            shares[0],
            shares[1],
            shares[2],
            shares[3],
            shares[4],
            shares[5],
            shares[6],
            shares[7],
            shares[8],
        ),
        "rep",
    )


def body(
    tokens,
    block_order,
    attn_gain,
    q_weight,
    k_weight,
    v_weight,
    o_weight,
    ffn_gain,
    gate_weight,
    up_weight,
    down_weight,
    cotangent,
):
    row_count = tokens.shape[0]
    order_row = block_order[0]
    own_block = lax.dynamic_index_in_dim(order_row, lax.axis_index("shard"), 0, keepdims=False)
    local_index = jnp.arange(row_count, dtype=jnp.int32)
    q_positions = own_block * row_count + local_index
    key_positions = (order_row[:, None] * row_count + local_index[None, :]).reshape(-1)
    cos_table, sin_table = rope_tables(q_positions, HD)
    params = (
        attn_gain,
        q_weight,
        k_weight,
        v_weight,
        o_weight,
        ffn_gain,
        gate_weight,
        up_weight,
        down_weight,
    )
    hidden = tokens.astype(jnp.float32)
    kept_weights = []
    layer_index = 0
    gathered = gather_forward(params, layer_index)
    hidden, saved = layer_forward(
        hidden, gathered, q_positions, key_positions, cos_table, sin_table
    )
    saved_list = [saved]
    kept_weights.append(gathered)
    gradient = cotangent.astype(jnp.float32)
    reduced = [None] * LAYERS
    for layer_index in reversed(range(LAYERS)):
        gathered = gather_backward(params, layer_index)
        gradient, terms = layer_backward(
            gradient,
            saved_list[layer_index],
            gathered,
            q_positions,
            key_positions,
            cos_table,
            sin_table,
        )
        shares = replica_sum(share_terms(terms))
        reduced[layer_index] = shares
    stacked = tuple((jnp.stack([reduced[0][member]]) for member in range(9)))
    return (
        hidden,
        gradient,
        stacked[0],
        stacked[1],
        stacked[2],
        stacked[3],
        stacked[4],
        stacked[5],
        stacked[6],
        stacked[7],
        stacked[8],
    )


def solution(mesh):
    placed = (
        P(("rep", "shard"), None),
        P("rep", None),
        P(None, "shard"),
        P(None, "shard", None),
        P(None, "shard", None),
        P(None, "shard", None),
        P(None, "shard", None),
        P(None, "shard"),
        P(None, "shard", None),
        P(None, "shard", None),
        P(None, "shard", None),
        P(("rep", "shard"), None),
    )
    return jax.shard_map(
        body,
        mesh=mesh,
        in_specs=placed,
        out_specs=(
            P(("rep", "shard"), None),
            P(("rep", "shard"), None),
            P(None, "shard"),
            P(None, "shard", None),
            P(None, "shard", None),
            P(None, "shard", None),
            P(None, "shard", None),
            P(None, "shard"),
            P(None, "shard", None),
            P(None, "shard", None),
            P(None, "shard", None),
        ),
        check_vma=False,
    )
```

profile of v0, /device:TPU:25, one launch (start us, length us, event | category | flops | bytes accessed | tf_op | source)
XLA Modules:
  0.0 570.6 jit_solution(2192590011341929955)
XLA Ops:
  13.4 3.8 all-reduce.7
  17.2 7.9 %all-gather.2 = bf16[1,576,192]{2,1,0:T(8,128)(2,1)S(1)} all-gather(bf16[1,288,192]{2,1,0:T(8,128)(2,1)S(1)} %copy-done.47), channel_id=4, replica_groups=mesh['rep'=16,'shard'=2] {'shard'}, dimensions={1}, use_global_device_ids=true | all-gather | bytes 331776 | tf_op jit(solution)/shard_map/all_gather | solution.py:71
  25.7 5.6 all_gather.46
  31.3 8.5 %all-gather.1 = bf16[1,576,192]{2,1,0:T(8,128)(2,1)S(1)} all-gather(bf16[1,288,192]{2,1,0:T(8,128)(2,1)S(1)} %copy-done.48), channel_id=3, replica_groups=mesh['rep'=16,'shard'=2] {'shard'}, dimensions={1}, use_global_device_ids=true | all-gather | bytes 331776 | tf_op jit(solution)/shard_map/all_gather | solution.py:72
  40.5 5.1 all_gather.44
  45.6 7.3 %all-gather.3 = bf16[1,576,576]{2,1,0:T(8,128)(2,1)S(1)} all-gather(bf16[1,288,576]{2,1,0:T(8,128)(2,1)S(1)} %copy-done.34), channel_id=5, replica_groups=mesh['rep'=16,'shard'=2] {'shard'}, dimensions={1}, use_global_device_ids=true | all-gather | bytes 995328 | tf_op jit(solution)/shard_map/all_gather | solution.py:70
  53.6 14.2 %all-gather.4 = bf16[1,576,576]{2,1,0:T(8,128)(2,1)S(1)} all-gather(bf16[1,288,576]{2,1,0:T(8,128)(2,1)S(1)} %copy-done.35), channel_id=6, replica_groups=mesh['rep'=16,'shard'=2] {'shard'}, dimensions={1}, use_global_device_ids=true | all-gather | bytes 995328 | tf_op jit(solution)/shard_map/all_gather | solution.py:73
  70.0 2.9 fusion
  72.8 11.9 %all-gather.15.cloned.1.call-done = bf16[1,576,1536]{2,1,0:T(8,128)(2,1)} async-done(((bf16[1,288,1536]{2,1,0:T(8,128)(2,1)}), bf16[1,576,1536]{2,1,0:T(8,128)(2,1)}) %all-gather.15.cloned.1.call-update) | async-done | bytes 1769488 | tf_op jit(solution)/shard_map/all_gather | solution.py:76
  84.7 2.9 fusion.6
  87.6 29.2 %all-gather.13.cloned.1.call-done = bf16[1,576,1536]{2,1,0:T(8,128)(2,1)} async-done(((bf16[1,288,1536]{2,1,0:T(8,128)(2,1)}), bf16[1,576,1536]{2,1,0:T(8,128)(2,1)}) %all-gather.13.cloned.1.call-update) | async-done | bytes 1769488 | tf_op jit(solution)/shard_map/all_gather | solution.py:75
  116.8 3.5 multiply_convert_fusion.1
  127.4 9.1 %reduce-scatter.12.cloned.1.call-done = f32[128,192]{0,1:T(8,128)} async-done(((f32[256,192]{0,1:T(8,128)}), f32[128,192]{0,1:T(8,128)}) %reduce-scatter.12.cloned.1.call-update) | async-done | bytes 98320 | tf_op jit(solution)/shard_map/reduce_scatter | solution.py:230
  138.6 11.6 %reduce-scatter.10.cloned.1.call-done = f32[128,192]{0,1:T(8,128)} async-done(((f32[256,192]{0,1:T(8,128)}), f32[128,192]{0,1:T(8,128)}) %reduce-scatter.10.cloned.1.call-update) | async-done | bytes 98320 | tf_op jit(solution)/shard_map/reduce_scatter | solution.py:227
  165.0 3.2 reduce-scatter.18.cloned.1.call-done
  168.2 18.2 %reduce-scatter.16.cloned.1.call-done = f32[288,192]{1,0:T(8,128)} async-done(((f32[576,192]{1,0:T(8,128)}), f32[288,192]{1,0:T(8,128)}) %reduce-scatter.16.cloned.1.call-update) | async-done | bytes 221200 | tf_op jit(solution)/shard_map/reduce_scatter | solution.py:263
  186.4 27.8 %reduce-scatter.20.cloned.1.call-done = f32[288,576]{1,0:T(8,128)} async-done(((f32[576,576]{1,0:T(8,128)}), f32[288,576]{1,0:T(8,128)}) %reduce-scatter.20.cloned.1.call-update) | async-done | bytes 663568 | tf_op jit(solution)/shard_map/reduce_scatter | solution.py:265
  214.2 27.9 %reduce-scatter.14.cloned.1.call-done = f32[288,576]{1,0:T(8,128)} async-done(((f32[576,576]{1,0:T(8,128)}), f32[288,576]{1,0:T(8,128)}) %reduce-scatter.14.cloned.1.call-update) | async-done | bytes 663568 | tf_op jit(solution)/shard_map/reduce_scatter | solution.py:262
  242.1 49.8 %reduce-scatter.26.cloned.1.call-done = f32[768,576]{0,1:T(8,128)} async-done(((f32[1536,576]{0,1:T(8,128)}), f32[768,576]{0,1:T(8,128)}) %reduce-scatter.26.cloned.1.call-update) | async-done | bytes 1769488 | tf_op jit(solution)/shard_map/reduce_scatter | solution.py:269
  291.9 50.0 %reduce-scatter.22.cloned.1.call-done = f32[288,1536]{1,0:T(8,128)} async-done(((f32[576,1536]{1,0:T(8,128)}), f32[288,1536]{1,0:T(8,128)}) %reduce-scatter.22.cloned.1.call-update) | async-done | bytes 1769488 | tf_op jit(solution)/shard_map/reduce_scatter | solution.py:267
  342.0 49.8 %reduce-scatter.24.cloned.1.call-done = f32[288,1536]{1,0:T(8,128)} async-done(((f32[576,1536]{1,0:T(8,128)}), f32[288,1536]{1,0:T(8,128)}) %reduce-scatter.24.cloned.1.call-update) | async-done | bytes 1769488 | tf_op jit(solution)/shard_map/reduce_scatter | solution.py:268
  396.6 3.8 all-reduce.6
  400.6 27.5 %all-reduce.4 = (f32[1,288]{1,0:T(1,128)}, f32[1,288]{1,0:T(1,128)}) all-reduce(f32[1,288]{1,0:T(1,128)S(1)} %stack.27, f32[1,288]{1,0:T(1,128)S(1)} %stack.32), channel_id=1, replica_groups=mesh['rep'=16,'shard'=2] {'rep'}, use_global_device_ids=true, to_apply=%region_10.11 | all-reduce | flops 576 | bytes 4608 | tf_op jit(solution)/shard_map/psum | solution.py:274
  428.9 125.3 %all-reduce.10.cloned.1.call-done = (f32[1,288,576]{2,1,0:T(8,128)}, f32[1,288,192]{2,1,0:T(8,128)}, f32[1,288,192]{2,1,0:T(8,128)}, f32[1,288,576]{2,1,0:T(8,12...) async-done(((f32[1,288,576]{2,1,0:T(8,128)}, f32[1,288,192]{2,1,0:T(8,128)}, f32[1,288,192]{2,1,0:T(8,128)}, f32[1,288,576]{2,1,0:T(8,128)}, ...) | async-done | bytes 7077904 | tf_op jit(solution)/shard_map/psum | solution.py:274
  (223 shorter events, 47.9 us)
Async XLA Ops:
  7.2 62.7 %all-gather.17.cloned.1.call-start = ((), (), s32[]{:S(2)}) async-start(), calls=%async_computation.20 | async-start | bytes 2654208 | tf_op jit(solution)/shard_map/all_gather | solution.py:77
  8.0 76.7 %all-gather.15.cloned.1.call-start = ((), (), s32[]{:S(2)}) async-start(), calls=%async_computation.19 | async-start | bytes 2654208 | tf_op jit(solution)/shard_map/all_gather | solution.py:76
  8.7 22.6 %copy-start.48 = (bf16[1,288,192]{2,1,0:T(8,128)(2,1)S(1)}, bf16[1,288,192]{2,1,0:T(8,128)(2,1)}, u32[]{:S(2)}) copy-start(bf16[1,288,192]{2,1,0:T(8,128)(2,1)} %param.17) | copy-start | bytes 331780
  8.7 108.1 %all-gather.13.cloned.1.call-start = ((), (), s32[]{:S(2)}) async-start(), calls=%async_computation.18 | async-start | bytes 2654208 | tf_op jit(solution)/shard_map/all_gather | solution.py:75
  9.5 36.2 %copy-start.34 = (bf16[1,288,576]{2,1,0:T(8,128)(2,1)S(1)}, bf16[1,288,576]{2,1,0:T(8,128)(2,1)}, u32[]{:S(2)}) copy-start(bf16[1,288,576]{2,1,0:T(8,128)(2,1)} %param.15) | copy-start | bytes 995332
  9.5 127.0 %reduce-scatter.12.cloned.1.call-start = ((), (), s32[]{:S(2)}) async-start(), calls=%async_computation.10 | async-start | bytes 294912 | tf_op jit(solution)/shard_map/reduce_scatter | solution.py:230
  11.7 41.2 %copy-start.53 = (f32[128]{0:T(128)}, f32[128]{0:T(128)S(1)}, u32[]{:S(2)}) copy-start(f32[128]{0:T(128)S(1)} %add_rsqrt_fusion.1) | copy-start | bytes 1540
  17.2 35.7 %copy-start.44 = (f32[576]{0:T(1024)}, f32[576]{0:T(1024)S(1)}, u32[]{:S(2)}) copy-start(f32[576]{0:T(1024)S(1)} %convert_element_type.100) | copy-start | bytes 6916
  17.2 52.5 %copy-start.49 = (f32[576]{0:T(1024)}, f32[576]{0:T(1024)S(1)}, u32[]{:S(2)}) copy-start(f32[576]{0:T(1024)S(1)} %convert_element_type.101) | copy-start | bytes 6916
  25.1 27.8 %copy-start.7 = (bf16[1,576,192]{2,1,0:T(8,128)(2,1)}, bf16[1,576,192]{2,1,0:T(8,128)(2,1)S(1)}, u32[]{:S(2)}) copy-start(bf16[1,576,192]{2,1,0:T(8,128)(2,1)S(1)} %all-gather.2) | copy-start | bytes 663556
  25.3 28.2 %copy-start.27 = (f32[128,32]{0,1:T(8,128)}, f32[128,32]{0,1:T(8,128)S(1)}, u32[]{:S(2)}) copy-start(f32[128,32]{0,1:T(8,128)S(1)} %get-tuple-element.40) | copy-start | bytes 49156
  31.3 36.6 %copy-start.31 = (bf16[256,192]{0,1:T(8,128)(2,1)}, bf16[256,192]{0,1:T(8,128)(2,1)S(1)}, u32[]{:S(2)}) copy-start(bf16[256,192]{0,1:T(8,128)(2,1)S(1)} %all_gather.46) | copy-start | bytes 294916
  45.6 22.9 %copy-start.29 = (bf16[256,192]{0,1:T(8,128)(2,1)}, bf16[256,192]{0,1:T(8,128)(2,1)S(1)}, u32[]{:S(2)}) copy-start(bf16[256,192]{0,1:T(8,128)(2,1)S(1)} %all_gather.44) | copy-start | bytes 294916
  87.6 32.7 %copy-start.1 = (bf16[1,576,1536]{2,1,0:T(8,128)(2,1)S(1)}, bf16[1,576,1536]{2,1,0:T(8,128)(2,1)}, u32[]{:S(2)}) copy-start(bf16[1,576,1536]{2,1,0:T(8,128)(2,1)} %all-gather.15.cloned.1.call-done) | copy-start | bytes 5308420
  125.4 24.7 %reduce-scatter.10.cloned.1.call-start = ((), (), s32[]{:S(2)}) async-start(), calls=%async_computation.9 | async-start | bytes 294912 | tf_op jit(solution)/shard_map/reduce_scatter | solution.py:227
  126.3 23.8 %copy-start.28 = (f32[128,32]{0,1:T(8,128)S(1)}, f32[128,32]{0,1:T(8,128)}, u32[]{:S(2)}) copy-start(f32[128,32]{0,1:T(8,128)} %copy-done.27) | copy-start | bytes 49156
  127.3 40.9 %reduce-scatter.18.cloned.1.call-start = ((), (), s32[]{:S(2)}) async-start(), calls=%async_computation.13 | async-start | bytes 884736 | tf_op jit(solution)/shard_map/reduce_scatter | solution.py:264
  138.5 47.9 %reduce-scatter.16.cloned.1.call-start = ((), (), s32[]{:S(2)}) async-start(), calls=%async_computation.12 | async-start | bytes 884736 | tf_op jit(solution)/shard_map/reduce_scatter | solution.py:263
  152.1 62.1 %reduce-scatter.20.cloned.1.call-start = ((), (), s32[]{:S(2)}) async-start(), calls=%async_computation.14 | async-start | bytes 2211840 | tf_op jit(solution)/shard_map/reduce_scatter | solution.py:265
  153.7 88.4 %reduce-scatter.14.cloned.1.call-start = ((), (), s32[]{:S(2)}) async-start(), calls=%async_computation.11 | async-start | bytes 2211840 | tf_op jit(solution)/shard_map/reduce_scatter | solution.py:262
  155.6 136.3 %reduce-scatter.26.cloned.1.call-start = ((), (), s32[]{:S(2)}) async-start(), calls=%async_computation.17 | async-start | bytes 5308416 | tf_op jit(solution)/shard_map/reduce_scatter | solution.py:269
  158.0 183.9 %reduce-scatter.22.cloned.1.call-start = ((), (), s32[]{:S(2)}) async-start(), calls=%async_computation.15 | async-start | bytes 5308416 | tf_op jit(solution)/shard_map/reduce_scatter | solution.py:267
  161.4 230.3 %reduce-scatter.24.cloned.1.call-start = ((), (), s32[]{:S(2)}) async-start(), calls=%async_computation.16 | async-start | bytes 5308416 | tf_op jit(solution)/shard_map/reduce_scatter | solution.py:268
  164.9 389.3 %all-reduce.10.cloned.1.call-start = ((), (), s32[]{:S(2)}) async-start(), calls=%async_computation.21 | async-start | bytes 14745600 | tf_op jit(solution)/shard_map/psum | solution.py:274
  (52 other events, 182.0 us)
Sparse Core Ops, SparseCore 0:
  9.6 37.9 all-gather.16
  49.2 35.4 all-gather.14
  86.3 30.5 all-gather.12
  125.5 10.9 reduce-scatter.11
  139.1 10.9 reduce-scatter.9
  152.8 15.3 reduce-scatter.17
  171.1 15.2 reduce-scatter.15
  189.2 24.9 reduce-scatter.19
  217.1 24.9 reduce-scatter.13
  244.2 47.6 reduce-scatter.25
  294.3 47.6 reduce-scatter.21
  344.1 47.6 reduce-scatter.23
  397.1 157.0 all-reduce.9
where the time goes:
time: 574 us; the launch traced here: 571 us
  waiting for transfers between devices  416 us (72%)
  blocking collectives  83.6 us (15%)
  matrix products  33.3 us (6%)
  local copies, waits for them, and re-layouts  16.2 us (3%)
  between operations  16.1 us (3%)
    psum x1, waiting for transfers between devices, replica_sum(): lax.psum((shares[0], shares[1], shares[2], shares[3], shares[4], shares[5...  125 us
    reduce_scatter x1, waiting for transfers between devices, share_terms(): lax.psum_scatter(terms[6], 'shard', scatter_dimension=0, tiled=True)  50 us
    reduce_scatter x1, waiting for transfers between devices, share_terms(): lax.psum_scatter(terms[7], 'shard', scatter_dimension=0, tiled=True)  49.8 us
    reduce_scatter x1, waiting for transfers between devices, share_terms(): lax.psum_scatter(terms[8], 'shard', scatter_dimension=0, tiled=True)  49.8 us
    all_gather x1, waiting for transfers between devices, gather_forward(): lax.all_gather(params[6][layer_index], 'shard', axis=0, tiled=True)  29.2 us
    reduce_scatter x1, waiting for transfers between devices, share_terms(): lax.psum_scatter(terms[1], 'shard', scatter_dimension=0, tiled=True)  27.9 us
    reduce_scatter x1, waiting for transfers between devices, share_terms(): lax.psum_scatter(terms[4], 'shard', scatter_dimension=0, tiled=True)  27.8 us
    psum x1, blocking collectives, replica_sum(): lax.psum((shares[0], shares[1], shares[2], shares[3], shares[4], shares[5...  27.5 us
  transfers between devices with their start and end apart: 13, of which 12 were waited for; matrix products, arithmetic and copies ran while one was open for 6% of the time, Pallas kernels for 0%

commit v1 on v0

--- a/solution.py
+++ b/solution.py
@@ -3,6 +3,8 @@
 import jax
 import jax.numpy as jnp
 from jax import lax
+from jax.experimental import pallas as pl
+from jax.experimental.pallas import tpu as pltpu
 from jax.sharding import PartitionSpec as P
 
 H = 9
@@ -359,6 +361,475 @@
     )
 
 
+F32 = jnp.float32
+BF16 = jnp.bfloat16
+MESH = pl.DeviceIdType.MESH
+
+
+def nn(left, right):
+    return lax.dot_general(left, right, (((1,), (0,)), ((), ())), preferred_element_type=F32)
+
+
+def nt(left, right):
+    return lax.dot_general(left, right, (((1,), (1,)), ((), ())), preferred_element_type=F32)
+
+
+def tn(left, right):
+    return lax.dot_general(left, right, (((0,), (0,)), ((), ())), preferred_element_type=F32)
+
+
+def swap_halves(x):
+    width = x.shape[-1]
+    lane = lax.broadcasted_iota(jnp.int32, x.shape, 1)
+    return jnp.where(
+        lane % HD < HD // 2, pltpu.roll(x, width - HD // 2, 1), pltpu.roll(x, HD // 2, 1)
+    )
+
+
+def fused_kernel(
+    tok_ref, cot_ref, cos_ref, sin_ref, bias_ref, gain_ref, wa_ref, gate_ref, up_ref, down_ref,
+    out_ref, gin_ref, o1_ref, o2_ref, o3_ref,
+    wa, wg, wu, gain_in, cot, kv, bb, part_out, part_in, dbo, dbi, probs, a_half, t_half, dm_x,
+    dkv_out, dkv_in, dqk_x, dv_x, gg_out, gg_in, g1, g2, g3, r1a, r1b, r1c, r2a, r2b, r2c,
+    r3a, r3b, r3c, f1, f2, f3, send_sem, recv_sem, local_sem,
+):
+    rows = tok_ref.shape[0]
+    rep = lax.axis_index("rep")
+    s = lax.axis_index("shard")
+    core = rep % 2
+    y = (rep // 2) % 2
+    z = rep // 4
+    xpeer = (rep, 1 - s)
+    cpeer = (rep + 1 - 2 * core, s)
+    ypeer = (rep + 2 - 4 * y, s)
+
+    def zdev(z2):
+        return (z2 * 4 + y * 2 + core, s)
+
+    zpeers = [zdev((z + d) % 4) for d in (1, 2, 3)]
+    counter = [0]
+    started = []
+
+    def remote(src, dst, device):
+        i = counter[0]
+        counter[0] += 1
+        c = pltpu.make_async_remote_copy(
+            src_ref=src, dst_ref=dst, send_sem=send_sem.at[i], recv_sem=recv_sem.at[i],
+            device_id=device, device_id_type=MESH,
+        )
+        c.start()
+        started.append(c)
+        return c
+
+    half = wa_ref.shape[0]
+    ffh = wg.shape[1]
+    mine = pl.multiple_of(s * half, 16)
+    theirs = pl.multiple_of((1 - s) * half, 16)
+    local = [
+        pltpu.make_async_copy(wa_ref, wa.at[pl.ds(mine, half), :], local_sem.at[0]),
+        pltpu.make_async_copy(
+            gate_ref.at[:, pl.ds(pl.multiple_of(s * ffh, 128), ffh)],
+            wg.at[pl.ds(mine, half), :], local_sem.at[1],
+        ),
+        pltpu.make_async_copy(
+            up_ref.at[:, pl.ds(pl.multiple_of(s * ffh, 128), ffh)],
+            wu.at[pl.ds(mine, half), :], local_sem.at[2],
+        ),
+    ]
+    for c in local:
+        c.start()
+
+    barrier = pltpu.get_barrier_semaphore()
+    for peer in [xpeer, cpeer, ypeer] + zpeers:
+        pl.semaphore_signal(barrier, inc=1, device_id=peer, device_id_type=MESH)
+    pl.semaphore_wait(barrier, 6)
+
+    gain_copy = remote(gain_ref, gain_in, xpeer)
+    hr = half // 2
+    targets = [(wa_ref, wa, 0), (gate_ref, wg, ffh), (up_ref, wu, ffh)]
+    xcopies = []
+    for src, dst, other in targets:
+        hc = dst.shape[1] // 2
+        xcopies.append(
+            remote(
+                src.at[
+                    pl.ds(pl.multiple_of(y * hr, 16), hr),
+                    pl.ds(pl.multiple_of((1 - s) * other + core * hc, 128), hc),
+                ],
+                dst.at[
+                    pl.ds(pl.multiple_of(s * half + y * hr, 16), hr),
+                    pl.ds(pl.multiple_of(core * hc, 128), hc),
+                ],
+                xpeer,
+            )
+        )
+    cot_copy = remote(cot_ref, cot, xpeer)
+
+    def ystep(i):
+        dst = targets[i][1]
+        hc = dst.shape[1] // 2
+        xcopies[i].wait_recv()
+        block = dst.at[
+            pl.ds(pl.multiple_of((1 - s) * half + y * hr, 16), hr),
+            pl.ds(pl.multiple_of(core * hc, 128), hc),
+        ]
+        return remote(block, block, ypeer)
+
+    def cstep(i, ycopy):
+        dst = targets[i][1]
+        hc = dst.shape[1] // 2
+        ycopy.wait_recv()
+        block = dst.at[
+            pl.ds(theirs, half), pl.ds(pl.multiple_of(core * hc, 128), hc)
+        ]
+        return remote(block, block, cpeer)
+
+    ya = ystep(0)
+    hidden = tok_ref[...].astype(F32)
+    rr = lax.rsqrt(jnp.mean(hidden * hidden, axis=-1, keepdims=True) + norm_eps)
+    normed = hidden * rr
+    gain_copy.wait_recv()
+    gains = gain_ref[...].astype(F32) + gain_in[...].astype(F32)
+    attn_g = gains[0:1, :]
+    ffn_g = gains[1:2, :]
+    attn_in = (normed * attn_g).astype(BF16)
+    yg = ystep(1)
+    ca = cstep(0, ya)
+    yu = ystep(2)
+    dm = attn_in.shape[1] // 2
+
+    def pick(value, flag):
+        return jnp.where(flag == 0, value[:, :dm], value[:, dm:])
+
+    for c in local:
+        c.wait()
+    ca.wait_recv()
+    qk = nn(attn_in, wa[:, :768])
+    cos_t = cos_ref[...]
+    sin_t = sin_ref[...]
+    qk = (qk * cos_t + swap_halves(qk) * sin_t).astype(BF16)
+    v = nn(attn_in, wa[:, 1280:1536])[:, 64:256].astype(BF16)
+    kv_own = jnp.concatenate([qk[:, 576:768], v], axis=1)
+    kv[0] = kv_own
+    kv_copy = remote(kv.at[0], kv.at[1], xpeer)
+    a_half[0] = pick(attn_in, s)
+    a_half[1] = pick(attn_in, 1 - s)
+    cg = cstep(1, yg)
+    cu = cstep(2, yu)
+    kv_copy.wait_recv()
+    kv_oth = kv[1]
+    groups = H // KV
+    bias = bias_ref[...]
+    bias3 = jnp.concatenate([bias] * groups, axis=0)
+
+    def stack(value, g):
+        return jnp.concatenate(
+            [value[:, HD * j : HD * (j + 1)] for j in range(g * groups, (g + 1) * groups)], axis=0
+        )
+
+    def unstack(values):
+        return [v[i * rows : (i + 1) * rows] for v in values for i in range(groups)]
+
+    def keys(off, g):
+        lo = off + HD * g
+        return jnp.concatenate([kv_own[:, lo : lo + HD], kv_oth[:, lo : lo + HD]], axis=0)
+
+    qs = [stack(qk, g) for g in range(KV)]
+    ks = [keys(0, g) for g in range(KV)]
+    vs = [keys(KV * HD, g) for g in range(KV)]
+    outs = []
+    for g in range(KV):
+        sc = nt(qs[g], ks[g]) * HD ** (-0.5) + bias3
+        top = jnp.max(sc, axis=-1, keepdims=True)
+        lse = top + jnp.log(jnp.sum(jnp.exp(sc - top), axis=-1, keepdims=True))
+        p = jnp.exp(sc - lse)
+        probs[g] = p
+        outs.append(nn(p.astype(BF16), vs[g]).astype(BF16))
+    attended = jnp.concatenate(unstack(outs), axis=1)
+    w_o = wa[:, 768:1344]
+    middle = hidden + nn(attended, w_o)
+    rr2 = lax.rsqrt(jnp.mean(middle * middle, axis=-1, keepdims=True) + norm_eps)
+    normed2 = middle * rr2
+    bb[0:rows] = (normed2 * ffn_g).astype(BF16)
+    b_copy = remote(bb.at[pl.ds(0, rows)], bb.at[pl.ds(rows, rows)], xpeer)
+    t_half[0] = pick(attended, s)
+    t_half[1] = pick(attended, 1 - s)
+    a_copy = remote(a_half.at[1], a_half.at[2], xpeer)
+    cot_copy.wait_recv()
+    grad_all = jnp.concatenate([cot_ref[...], cot[...]], axis=0)
+    d_mix = nt(grad_all, down_ref[...])
+    cg.wait_recv()
+    cu.wait_recv()
+    b_copy.wait_recv()
+    ball = bb[...]
+    gt = nn(ball, wg[...])
+    up = nn(ball, wu[...])
+    sig = jax.nn.sigmoid(gt)
+    silu = gt * sig
+    mix = (silu * up).astype(BF16)
+    d_up = (d_mix * silu).astype(BF16)
+    d_gt = (d_mix * up * sig * (1.0 + gt * (1.0 - sig))).astype(BF16)
+    db = nt(d_gt, wg[...]) + nt(d_up, wu[...])
+    dbo[...] = db[rows:].astype(BF16)
+    db_copy = remote(dbo, dbi, xpeer)
+    part = nn(mix, down_ref[...])
+    part_out[...] = part[rows:].astype(BF16)
+    part_copy = remote(part_out, part_in, xpeer)
+    t_copy = remote(t_half.at[1], t_half.at[2], xpeer)
+
+    gs, r1, r2, r3 = (g2, g1, g3), (r1b, r1a, r1c), (r2b, r2a, r2c), (r3b, r3a, r3c)
+    fs, res = (f2, f1, f3), (o2_ref, o1_ref, o3_ref)
+    state = [None] * 3
+
+    def rs_core(p):
+        state[p] = remote(gs[p].at[pl.ds((1 - core) * 8, 8)], r1[p], cpeer)
+
+    def rs_y(p):
+        state[p].wait_recv()
+
+        @pl.loop(0, 8)
+        def _(k):
+            r1[p][k] = (r1[p][k].astype(F32) + gs[p][core * 8 + k].astype(F32)).astype(BF16)
+
+        state[p] = remote(r1[p].at[pl.ds((1 - y) * 4, 4)], r2[p], ypeer)
+
+    def rs_z(p):
+        state[p].wait_recv()
+
+        @pl.loop(0, 4)
+        def _(k):
+            r2[p][k] = (r2[p][k].astype(F32) + r1[p][y * 4 + k].astype(F32)).astype(BF16)
+
+        state[p] = [
+            remote(r2[p].at[(z + d) % 4], r3[p].at[d - 1], zpeers[d - 1]) for d in (1, 2, 3)
+        ]
+
+    def ag_z(p):
+        for c in state[p]:
+            c.wait_recv()
+        total = r2[p][z].astype(F32)
+        for d in range(3):
+            total = total + r3[p][d].astype(F32)
+        slot = core
+        if p == 1:
+            fs[p][0] = total.astype(BF16)
+            i = counter[0]
+            counter[0] += 1
+            swap = pltpu.make_async_remote_copy(
+                src_ref=fs[p].at[0], dst_ref=fs[p].at[1], send_sem=send_sem.at[i],
+                recv_sem=recv_sem.at[i], device_id=xpeer, device_id_type=MESH,
+            )
+
+            @pl.when(core == 1)
+            def _():
+                swap.start()
+                swap.wait()
+                fs[p][0] = fs[p][1]
+
+            slot = jnp.where(s == 0, core, 1 - core)
+            res[p][slot * 8 + y * 4 + z] = fs[p][0]
+        else:
+            fs[p][0] = total.astype(BF16)
+            res[p][slot * 8 + y * 4 + z] = fs[p][0]
+        place = slot * 8 + y * 4 + z
+        state[p] = [
+            remote(fs[p].at[0], res[p].at[place], zpeers[d - 1]) for d in (1, 2, 3)
+        ]
+        return slot
+
+    slots = [None] * 3
+
+    def ag_y(p):
+        for c in state[p]:
+            c.wait_recv()
+        block = res[p].at[pl.ds(slots[p] * 8 + y * 4, 4)]
+        state[p] = remote(block, block, ypeer)
+
+    def ag_core(p):
+        state[p].wait_recv()
+        block = res[p].at[pl.ds(slots[p] * 8, 8)]
+        state[p] = remote(block, block, cpeer)
+
+    g2[...] = tn(mix, grad_all).astype(BF16).reshape(g2.shape)
+    rs_core(0)
+    for half_t, dd in enumerate((d_gt, d_up)):
+        gw = tn(ball, dd).astype(BF16)
+        for h in range(2):
+            for yy in range(2):
+                for zz in range(2):
+                    k = jnp.where(s == h, 0, 8) + yy * 4 + half_t * 2 + zz
+                    lo = h * half + yy * hr
+                    g1[k] = gw[lo : lo + hr, zz * 384 : (zz + 1) * 384]
+    rs_core(1)
+    db_copy.wait_recv()
+    db = db[:rows] + dbi[...].astype(F32)
+    gain2 = jnp.sum(db * normed2, axis=0, keepdims=True)
+    e = db * ffn_g
+    dm1 = cot_ref[...].astype(F32) + rr2 * (
+        e - normed2 * jnp.mean(e * normed2, axis=-1, keepdims=True)
+    )
+    dm1b = dm1.astype(BF16)
+    dm_x[0] = dm1b
+    dm_copy = remote(dm_x.at[0], dm_x.at[1], xpeer)
+    d_att = nt(dm1b, w_o).astype(BF16)
+    rs_y(0)
+    part_copy.wait_recv()
+    out_ref[...] = middle + part[:rows] + part_in[...].astype(F32)
+
+    dqs, dks, dvs = [], [], []
+    for g in range(KV):
+        do_g = stack(d_att, g)
+        p = probs[g]
+        dvs.append(tn(p.astype(BF16), do_g))
+        delta = jnp.sum(do_g.astype(F32) * outs[g].astype(F32), axis=-1, keepdims=True)
+        ds = (p * (nt(do_g, vs[g]) - delta) * HD ** (-0.5)).astype(BF16)
+        dqs.append(nn(ds, ks[g]))
+        dks.append(tn(ds, qs[g]))
+        if g == 0:
+            rs_y(1)
+    dkv = jnp.concatenate(dks + dvs, axis=1)
+    dkv_out[...] = dkv[rows:].astype(BF16)
+    dkv_copy = remote(dkv_out, dkv_in, xpeer)
+    rs_z(0)
+    dkv_copy.wait_recv()
+    dkv = dkv[:rows] + dkv_in[...].astype(F32)
+    dqk = jnp.concatenate(unstack(dqs) + [dkv[:, : KV * HD]], axis=1)
+    dqk = (dqk * cos_t - swap_halves(dqk) * sin_t).astype(BF16)
+    dvb = dkv[:, KV * HD :].astype(BF16)
+    dqk_x[0] = dqk
+    dv_x[0] = dvb
+    dqk_copy = remote(dqk_x.at[0], dqk_x.at[1], xpeer)
+    dv_copy = remote(dv_x.at[0], dv_x.at[1], xpeer)
+    da = nt(dqk, wa[:, :768]) + nt(
+        jnp.concatenate([jnp.zeros((rows, 64), BF16), dvb], axis=1), wa[:, 1280:1536]
+    )
+    gain1 = jnp.sum(da * normed, axis=0, keepdims=True)
+    gg_out[...] = jnp.concatenate([gain1, gain2, jnp.zeros((6, gain1.shape[1]), F32)], axis=0)
+    gg_copy = remote(gg_out, gg_in, xpeer)
+    rs_z(1)
+    f = da * attn_g
+    gin_ref[...] = dm1 + rr * (f - normed * jnp.mean(f * normed, axis=-1, keepdims=True))
+    for c in (a_copy, t_copy, dm_copy, dqk_copy, dv_copy):
+        c.wait_recv()
+    a_all = jnp.concatenate([a_half[0], a_half[2]], axis=0)
+    t_all = jnp.concatenate([t_half[0], t_half[2]], axis=0)
+    gw_o = tn(t_all, jnp.concatenate([dm_x[0], dm_x[1]], axis=0)).astype(BF16)
+    gw_qk = tn(a_all, jnp.concatenate([dqk_x[0], dqk_x[1]], axis=0)).astype(BF16)
+    gw_v = tn(a_all, jnp.concatenate([dv_x[0], dv_x[1]], axis=0)).astype(BF16)
+    columns = [
+        gw_qk[:, :384], gw_qk[:, 384:], gw_o[:, :384],
+        jnp.concatenate([gw_o[:, 384:], gw_v], axis=1),
+    ]
+    gg_copy.wait_recv()
+    gg = pick(gg_out[...] + gg_in[...], s)
+    gg = jnp.concatenate([gg, jnp.zeros((8, 384 - dm), F32)], axis=1)
+    row32 = lax.broadcasted_iota(jnp.int32, (32, 384), 0)
+    for cc in range(4):
+        for r in range(3):
+            g3[r * 4 + cc] = columns[cc][r * 80 : (r + 1) * 80]
+        g3[12 + cc, 0:48] = columns[cc][240:288]
+        if cc < 2:
+            tail = jnp.where(row32 == 0, jnp.broadcast_to(gg[cc : cc + 1], (32, 384)), 0.0)
+        else:
+            tail = jnp.zeros((32, 384), F32)
+        g3[12 + cc, 48:80] = tail.astype(BF16)
+    rs_core(2)
+    slots[0] = ag_z(0)
+    rs_y(2)
+    slots[1] = ag_z(1)
+    rs_z(2)
+    ag_y(0)
+    slots[2] = ag_z(2)
+    ag_y(1)
+    ag_core(0)
+    ag_y(2)
+    ag_core(1)
+    ag_core(2)
+    for st in state:
+        st.wait_recv()
+    for c in started:
+        c.wait_send()
+
+
+def fused_body(
+    tokens, block_order, attn_gain, q_weight, k_weight, v_weight, o_weight, ffn_gain,
+    gate_weight, up_weight, down_weight, cotangent,
+):
+    rows, width = tokens.shape
+    s = lax.axis_index("shard")
+    half = attn_gain.shape[1]
+    ff = gate_weight.shape[2]
+    order = block_order[0]
+    own = lax.dynamic_index_in_dim(order, s, 0, keepdims=False)
+    other = lax.dynamic_index_in_dim(order, 1 - s, 0, keepdims=False)
+    index = jnp.arange(rows, dtype=jnp.int32)
+    q_pos = own * rows + index
+    k_pos = jnp.concatenate([q_pos, other * rows + index])
+    bias = jnp.where(k_pos[None, :] <= q_pos[:, None], 0.0, -1e30).astype(F32)
+    cos_t, sin_t = rope_tables(q_pos, HD)
+    cos_t, sin_t = cos_t[:, 0], sin_t[:, 0]
+    cos_t = jnp.tile(cos_t, (1, 2 * (H + KV)))
+    sin_t = jnp.tile(jnp.concatenate([-sin_t, sin_t], axis=1), (1, H + KV))
+    gains = jnp.concatenate([attn_gain, ffn_gain, jnp.zeros((14, half), BF16)], axis=0)
+    gains = jnp.concatenate(
+        [jnp.where(s == 0, gains, 0), jnp.where(s == 1, gains, 0)], axis=1
+    ).astype(BF16)
+    wa = jnp.concatenate([q_weight[0], k_weight[0], o_weight[0], v_weight[0]], axis=1)
+    vm = pl.BlockSpec(memory_space=pltpu.VMEM)
+    shapes = [(144, 384), (48, width), (80, 384)]
+
+    def buf(*shape, dtype=BF16):
+        return pltpu.VMEM(shape, dtype)
+
+    scratch = [
+        buf(width, 1536), buf(width, ff // 2), buf(width, ff // 2), buf(16, width),
+        buf(rows, width), buf(2, rows, 384), buf(2 * rows, width), buf(rows, width),
+        buf(rows, width), buf(rows, width), buf(rows, width),
+        buf(KV, 3 * rows, 2 * rows, dtype=F32), buf(3, rows, half), buf(3, rows, half),
+        buf(2, rows, width), buf(rows, 384), buf(rows, 384), buf(2, rows, 768),
+        buf(2, rows, 192), buf(8, width, dtype=F32), buf(8, width, dtype=F32),
+    ]
+    for count in (16, 8, 4, 3, 2):
+        scratch += [buf(count, *sh) for sh in shapes]
+    scratch += [
+        pltpu.SemaphoreType.DMA((64,)), pltpu.SemaphoreType.DMA((64,)),
+        pltpu.SemaphoreType.DMA((3,)),
+    ]
+    block_out, input_grad, o1, o2, o3 = pl.pallas_call(
+        fused_kernel,
+        out_shape=(
+            jax.ShapeDtypeStruct((rows, width), F32),
+            jax.ShapeDtypeStruct((rows, width), F32),
+            *[jax.ShapeDtypeStruct((16, *sh), BF16) for sh in shapes],
+        ),
+        in_specs=[vm] * 10,
+        out_specs=[vm] * 5,
+        scratch_shapes=scratch,
+        compiler_params=pltpu.CompilerParams(
+            collective_id=0, has_side_effects=True, vmem_limit_bytes=56 * 1024 * 1024
+        ),
+    )(
+        tokens, cotangent, cos_t, sin_t, bias, gains, wa, gate_weight[0], up_weight[0],
+        down_weight[0],
+    )
+    gu = o1.reshape(2, 2, 2, 2, 144, 384)
+    gu = gu.transpose(2, 1, 4, 0, 3, 5).reshape(2, half, ff).astype(F32)
+    rest = o3.reshape(4, 4, 80, 384).transpose(0, 2, 1, 3).reshape(320, 1536).astype(F32)
+    return (
+        block_out,
+        input_grad,
+        rest[288:289, :288],
+        rest[None, :288, :576],
+        rest[None, :288, 576:768],
+        rest[None, :288, 1344:],
+        rest[None, :288, 768:1344],
+        rest[288:289, 384 : 384 + 288],
+        gu[0:1],
+        gu[1:2],
+        o2.reshape(1, 768, width).astype(F32),
+    )
+
+
 def solution(mesh):
     placed = (
         P(("rep", "shard"), None),
@@ -374,8 +845,9 @@
         P(None, "shard", None),
         P(("rep", "shard"), None),
     )
+    fused = mesh.shape["shard"] == 2 and mesh.shape["rep"] == 16
     return jax.shard_map(
-        body,
+        fused_body if fused else body,
         mesh=mesh,
         in_specs=placed,
         out_specs=(

time: 574 us -> 137 us (0.24)
  waiting for transfers between devices: 416 us -> 0 us
  Pallas kernels: 0 us -> 109 us
  blocking collectives: 83.6 us -> 0 us
  matrix products: 33.3 us -> 0 us
  between operations: 16.1 us -> 2.18 us
    reduce_scatter x9 -> x0, waiting for transfers between devices: 247 us -> none  [the longest x1 50 us: share_terms(): lax.psum_scatter(terms[6], 'shard', scatter_dimension=0, tiled=True)]
    psum x1 -> x0, waiting for transfers between devices: 125 us -> none  [replica_sum(): lax.psum((shares[0], shares[1], shares[2], shares[3], shares[4], shares[5...]
    pallas_call x0 -> x1, Pallas kernels: none -> 109 us  [fused_body(): pl.pallas_call(fused_kernel, out_shape=(jax.ShapeDtypeStruct((rows, width...]
    all_gather x6 -> x0, blocking collectives: 48.5 us -> none  [the longest x1 14.2 us: gather_forward(): lax.all_gather(params[4][layer_index], 'shard', axis=0, tiled=True)]
    all_gather x3 -> x0, waiting for transfers between devices: 41.1 us -> none  [the longest x1 29.2 us: gather_forward(): lax.all_gather(params[6][layer_index], 'shard', axis=0, tiled=True)]
    dot_general x27 -> x0, matrix products: 33.3 us -> none  [the longest x7 13.3 us: transposed_product(): jnp.einsum('tk,tn->kn', left, right, preferred_element_type=jnp.float32)]
    psum x1 -> x0, blocking collectives: 27.5 us -> none  [replica_sum(): lax.psum((shares[0], shares[1], shares[2], shares[3], shares[4], shares[5...]
    unnamed x140 -> x33, local copies, waits for them, and re-layouts: 16.2 us -> 6.56 us
  transfers between devices with their start and end apart: 13 -> 0, of which waited for: 12 -> 0; matrix products, arithmetic and copies ran while one was open for 6% -> 0% of each run, Pallas kernels for 0% -> 0%
where the time goes in v1:
time: 137 us
  Pallas kernels  109 us (80%)
  local copies, waits for them, and re-layouts  21.9 us (16%)
  other arithmetic  3.66 us (3%)
  between operations  2.18 us (2%)
    pallas_call x1, Pallas kernels, fused_body(): pl.pallas_call(fused_kernel, out_shape=(jax.ShapeDtypeStruct((rows, width...  109 us
    unnamed x33, local copies, waits for them, and re-layouts  6.56 us
    slice x3, local copies, waits for them, and re-layouts, fused_body(): gu[1:2]  3.76 us
    slice x2, local copies, waits for them, and re-layouts, fused_body(): gu[0:1]  3.53 us

profile of v1, /device:TPU:25, one launch (start us, length us, event | category | flops | bytes accessed | tf_op | source)
XLA Modules:
  0.0 137.1 jit_solution(1025399376093029569)
XLA Ops:
  0.7 1.3 constant_dynamic-slice_fusion
  3.4 0.7 compare_select_fusion.bias_ref
  4.1 0.1 fusion
  4.4 0.9 copy.36.sin_ref
  5.3 0.9 copy.35.cos_ref
  6.4 0.7 pad_maximum_fusion.1.gain_ref
  7.1 1.3 copy.32
  8.4 1.2 concatenate.19.wa_ref
  9.6 0.8 copy.33.tok_ref
  10.4 0.8 copy.34.cot_ref
  11.2 109.4 %shard_map.203 = (f32[128,576]{1,0:T(8,128)}, f32[128,576]{1,0:T(8,128)}, bf16[16,144,384]{2,1,0:T(8,128)(2,1)}, bf16[16,48,576]{2,1,0:T(8,128)(2,1)}, bf16[16,80,384]{2,1,0:T(8,128)(2,1)}) custom-call(bf16[128,576]{1,0:T(8,128)(2,1)} %copy.33.tok_ref, bf16[128,576]{1,0:T(8,128)(2,1)} %copy.34.cot_ref, f32[128,768]{1,0:T(8,128)} %copy.35.cos_ref, ...), custom_call_target="tpu_custom_call" | custom-call | tf_op jit(solution)/shard_map/pallas_call | solution.py:798
  120.6 1.7 %convert_bitcast_fusion = f32[2,2,144,2,2,384]{5,2,4,0,1,3:T(8,128)S(1)} fusion(bf16[2,2,2,2,144,384]{5,4,3,2,1,0:T(8,128)(2,1)} %bitcast.39), kind=kLoop, calls=%fused_computation | loop fusion | flops 884736 | bytes 5308416 | tf_op jit(solution)/shard_map/convert_element_type | solution.py:816
  122.3 0.2 fusion.2
  122.6 0.9 copy.38
  123.5 2.6 %slice.37 = f32[1,288,1536]{2,1,0:T(8,128)} reshape(f32[1,2,144,2,2,384]{5,4,3,2,1,0:T(2,128)S(1)} %copy.38) | data formatting | bytes 3538944 | tf_op jit(solution)/shard_map/slice | solution.py:827
  126.1 0.9 copy.39
  127.0 2.6 %slice.39 = f32[1,288,1536]{2,1,0:T(8,128)} reshape(f32[1,2,144,2,2,384]{5,4,3,2,1,0:T(2,128)S(1)} %copy.39) | data formatting | bytes 3538944 | tf_op jit(solution)/shard_map/slice | solution.py:828
  129.8 0.8 copy.37
  130.7 1.2 slice_bitcast_fusion
  131.9 1.0 slice_bitcast_fusion.2
  133.0 0.6 fusion.3
  133.7 1.7 %copy.42 = f32[1,768,576]{1,2,0:T(8,128)} copy(f32[1,768,576]{2,1,0:T(8,128)S(1)} %bitcast_convert_fusion) | data formatting | bytes 3538944
  135.4 0.9 copy.40
  136.3 0.9 copy.41
  (39 shorter events, 0.7 us)
Async XLA Ops:
  0.6 5.7 %copy-start.12 = (bf16[1,288]{1,0:T(2,128)(2,1)S(1)}, bf16[1,288]{1,0:T(2,128)(2,1)}, u32[]{:S(2)}) copy-start(bf16[1,288]{1,0:T(2,128)(2,1)} %param.14) | copy-start | bytes 1732
  0.7 5.7 %copy-start.11 = (bf16[1,288]{1,0:T(2,128)(2,1)S(1)}, bf16[1,288]{1,0:T(2,128)(2,1)}, u32[]{:S(2)}) copy-start(bf16[1,288]{1,0:T(2,128)(2,1)} %param.19) | copy-start | bytes 1732
  0.7 6.4 %copy-start.2 = (bf16[1,768,576]{1,2,0:T(8,128)(2,1)S(1)}, bf16[1,768,576]{1,2,0:T(8,128)(2,1)}, u32[]{:S(2)}) copy-start(bf16[1,768,576]{1,2,0:T(8,128)(2,1)} %param.22) | copy-start | bytes 2654212
  4.3 4.1 %copy-start.3 = (bf16[1,288,576]{2,1,0:T(8,128)(2,1)S(1)}, bf16[1,288,576]{2,1,0:T(8,128)(2,1)}, u32[]{:S(2)}) copy-start(bf16[1,288,576]{2,1,0:T(8,128)(2,1)} %param.15) | copy-start | bytes 995332
  4.3 4.1 %copy-start.4 = (bf16[1,288,576]{2,1,0:T(8,128)(2,1)S(1)}, bf16[1,288,576]{2,1,0:T(8,128)(2,1)}, u32[]{:S(2)}) copy-start(bf16[1,288,576]{2,1,0:T(8,128)(2,1)} %param.18) | copy-start | bytes 995332
  4.3 4.1 %copy-start.9 = (bf16[1,288,192]{2,1,0:T(8,128)(2,1)S(1)}, bf16[1,288,192]{2,1,0:T(8,128)(2,1)}, u32[]{:S(2)}) copy-start(bf16[1,288,192]{2,1,0:T(8,128)(2,1)} %param.16) | copy-start | bytes 331780
  4.3 4.1 %copy-start.10 = (bf16[1,288,192]{2,1,0:T(8,128)(2,1)S(1)}, bf16[1,288,192]{2,1,0:T(8,128)(2,1)}, u32[]{:S(2)}) copy-start(bf16[1,288,192]{2,1,0:T(8,128)(2,1)} %param.17) | copy-start | bytes 331780
  6.2 3.3 %copy-start.7 = (bf16[128,576]{0,1:T(8,128)(2,1)S(1)}, bf16[128,576]{0,1:T(8,128)(2,1)}, u32[]{:S(2)}) copy-start(bf16[128,576]{0,1:T(8,128)(2,1)} %param.12) | copy-start | bytes 442372
  7.1 3.3 %copy-start.8 = (bf16[128,576]{0,1:T(8,128)(2,1)S(1)}, bf16[128,576]{0,1:T(8,128)(2,1)}, u32[]{:S(2)}) copy-start(bf16[128,576]{0,1:T(8,128)(2,1)} %param.23) | copy-start | bytes 442372
  127.0 2.6 %copy-start.1 = (bf16[16,80,384]{2,1,0:T(8,128)(2,1)S(1)}, bf16[16,80,384]{2,1,0:T(8,128)(2,1)}, u32[]{:S(2)}) copy-start(bf16[16,80,384]{2,1,0:T(8,128)(2,1)} %get-tuple-element.18) | copy-start | bytes 2949124
  130.7 2.8 %copy-start = (bf16[16,48,576]{2,1,0:T(8,128)(2,1)S(1)}, bf16[16,48,576]{2,1,0:T(8,128)(2,1)}, u32[]{:S(2)}) copy-start(bf16[16,48,576]{2,1,0:T(8,128)(2,1)} %get-tuple-element.20) | copy-start | bytes 2654212
  133.7 1.7 %copy-start.6 = (f32[128,576]{1,0:T(8,128)S(1)}, f32[128,576]{1,0:T(8,128)}, u32[]{:S(2)}) copy-start(f32[128,576]{1,0:T(8,128)} %get-tuple-element.32) | copy-start | bytes 884740
  133.7 2.6 %copy-start.5 = (f32[128,576]{1,0:T(8,128)S(1)}, f32[128,576]{1,0:T(8,128)}, u32[]{:S(2)}) copy-start(f32[128,576]{1,0:T(8,128)} %get-tuple-element.33) | copy-start | bytes 884740

commit v2 on v1

--- a/solution.py
+++ b/solution.py
@@ -387,9 +387,10 @@
 
 
 def fused_kernel(
-    tok_ref, cot_ref, cos_ref, sin_ref, bias_ref, gain_ref, wa_ref, gate_ref, up_ref, down_ref,
+    tok_hbm, order_ref, again_ref, q_hbm, k_hbm, v_hbm, o_hbm, fgain_ref, gate_hbm, up_hbm, down_hbm,
+    cot_hbm,
     out_ref, gin_ref, o1_ref, o2_ref, o3_ref,
-    wa, wg, wu, gain_in, cot, kv, bb, part_out, part_in, dbo, dbi, probs, a_half, t_half, dm_x,
+    tok_ref, cot_ref, down_ref, w5, w1, wg, wu, gain_ref, gain_in, cot, kv, bb, part_out, part_in, dbo, dbi, probs, a_half, t_half, dm_x,
     dkv_out, dkv_in, dqk_x, dv_x, gg_out, gg_in, g1, g2, g3, r1a, r1b, r1c, r2a, r2b, r2c,
     r3a, r3b, r3c, f1, f2, f3, send_sem, recv_sem, local_sem,
 ):
@@ -421,23 +422,51 @@
         started.append(c)
         return c
 
-    half = wa_ref.shape[0]
+    gate_ref, up_ref = gate_hbm.at[0], up_hbm.at[0]
+    half = gate_ref.shape[0]
     ffh = wg.shape[1]
     mine = pl.multiple_of(s * half, 16)
     theirs = pl.multiple_of((1 - s) * half, 16)
+    ffcols = pl.ds(pl.multiple_of(s * ffh, 128), ffh)
+    own_rows = pl.ds(mine, half)
+    pairs = [
+        (q_hbm.at[0], w5.at[0, own_rows]), (o_hbm.at[0], w5.at[1, own_rows]),
+        (k_hbm.at[0], w1.at[0, own_rows]), (v_hbm.at[0], w1.at[1, own_rows]),
+        (tok_hbm, tok_ref), (cot_hbm, cot_ref), (gate_ref.at[:, ffcols], wg.at[own_rows]),
+        (up_ref.at[:, ffcols], wu.at[own_rows]), (down_hbm.at[0], down_ref),
+    ]
     local = [
-        pltpu.make_async_copy(wa_ref, wa.at[pl.ds(mine, half), :], local_sem.at[0]),
-        pltpu.make_async_copy(
-            gate_ref.at[:, pl.ds(pl.multiple_of(s * ffh, 128), ffh)],
-            wg.at[pl.ds(mine, half), :], local_sem.at[1],
-        ),
-        pltpu.make_async_copy(
-            up_ref.at[:, pl.ds(pl.multiple_of(s * ffh, 128), ffh)],
-            wu.at[pl.ds(mine, half), :], local_sem.at[2],
-        ),
+        pltpu.make_async_copy(src, dst, local_sem.at[i]) for i, (src, dst) in enumerate(pairs)
     ]
     for c in local:
         c.start()
+
+    lane = lax.broadcasted_iota(jnp.int32, (rows, 128), 1)
+    sub = lax.broadcasted_iota(jnp.int32, (rows, 128), 0)
+    own, other = order_ref[0, s], order_ref[0, 1 - s]
+    position = own * rows + sub
+    frequency = jnp.exp((lane % (HD // 2)).astype(F32) * (-2.0 * math.log(rope_base) / HD))
+    angle = position.astype(F32) * frequency
+    cos_t = jnp.cos(angle)
+    sin_t = jnp.sin(angle)
+    sin_t = jnp.where(lane % HD < HD // 2, -sin_t, sin_t)
+    cos_t = jnp.concatenate([cos_t] * 6, axis=1)
+    sin_t = jnp.concatenate([sin_t] * 6, axis=1)
+    bias = jnp.concatenate(
+        [
+            jnp.where(start * rows + lane <= position, 0.0, -1e30).astype(F32)
+            for start in (own, other)
+        ],
+        axis=1,
+    )
+    both = jnp.concatenate([again_ref[...], fgain_ref[...]], axis=0).astype(F32)
+    none = jnp.zeros_like(both)
+    gain_ref[0:2] = jnp.where(
+        s == 0,
+        jnp.concatenate([both, none], axis=1),
+        jnp.concatenate([none, both], axis=1),
+    )
+    gain_ref[2:8] = jnp.zeros((6, 2 * half), F32)
 
     barrier = pltpu.get_barrier_semaphore()
     for peer in [xpeer, cpeer, ypeer] + zpeers:
@@ -445,81 +474,66 @@
     pl.semaphore_wait(barrier, 6)
 
     gain_copy = remote(gain_ref, gain_in, xpeer)
+    for c in local[:4]:
+        c.wait()
     hr = half // 2
-    targets = [(wa_ref, wa, 0), (gate_ref, wg, ffh), (up_ref, wu, ffh)]
-    xcopies = []
-    for src, dst, other in targets:
-        hc = dst.shape[1] // 2
-        xcopies.append(
-            remote(
-                src.at[
-                    pl.ds(pl.multiple_of(y * hr, 16), hr),
-                    pl.ds(pl.multiple_of((1 - s) * other + core * hc, 128), hc),
-                ],
-                dst.at[
-                    pl.ds(pl.multiple_of(s * half + y * hr, 16), hr),
-                    pl.ds(pl.multiple_of(core * hc, 128), hc),
-                ],
-                xpeer,
-            )
-        )
+    rows_x = pl.ds(pl.multiple_of(s * half + y * hr, 16), hr)
+    rows_y = pl.ds(pl.multiple_of(theirs + y * hr, 16), hr)
+    part_x = pl.ds(pl.multiple_of(y * hr, 16), hr)
+    hc = ffh // 2
+    cols = pl.ds(pl.multiple_of(core * hc, 128), hc)
+    cols_x = pl.ds(pl.multiple_of((1 - s) * ffh + core * hc, 128), hc)
+
+    def send(block, device):
+        return remote(block, block, device)
+
+    x5 = send(w5.at[core, rows_x], xpeer)
+    x1 = send(w1.at[core, rows_x], xpeer)
+    local[5].wait()
+    xg = remote(gate_ref.at[part_x, cols_x], wg.at[rows_x, cols], xpeer)
+    xu = remote(up_ref.at[part_x, cols_x], wu.at[rows_x, cols], xpeer)
     cot_copy = remote(cot_ref, cot, xpeer)
-
-    def ystep(i):
-        dst = targets[i][1]
-        hc = dst.shape[1] // 2
-        xcopies[i].wait_recv()
-        block = dst.at[
-            pl.ds(pl.multiple_of((1 - s) * half + y * hr, 16), hr),
-            pl.ds(pl.multiple_of(core * hc, 128), hc),
-        ]
-        return remote(block, block, ypeer)
-
-    def cstep(i, ycopy):
-        dst = targets[i][1]
-        hc = dst.shape[1] // 2
-        ycopy.wait_recv()
-        block = dst.at[
-            pl.ds(theirs, half), pl.ds(pl.multiple_of(core * hc, 128), hc)
-        ]
-        return remote(block, block, cpeer)
-
-    ya = ystep(0)
+    rows_c = pl.ds(theirs, half)
+
+    def forward(copy, block, device):
+        copy.wait_recv()
+        return send(block, device)
+
+    y5 = forward(x5, w5.at[core, rows_y], ypeer)
+    y1 = forward(x1, w1.at[core, rows_y], ypeer)
+    local[4].wait()
     hidden = tok_ref[...].astype(F32)
     rr = lax.rsqrt(jnp.mean(hidden * hidden, axis=-1, keepdims=True) + norm_eps)
     normed = hidden * rr
     gain_copy.wait_recv()
-    gains = gain_ref[...].astype(F32) + gain_in[...].astype(F32)
+    gains = gain_ref[...] + gain_in[...]
     attn_g = gains[0:1, :]
     ffn_g = gains[1:2, :]
     attn_in = (normed * attn_g).astype(BF16)
-    yg = ystep(1)
-    ca = cstep(0, ya)
-    yu = ystep(2)
+    c5 = forward(y5, w5.at[core, rows_c], cpeer)
+    c1 = forward(y1, w1.at[core, rows_c], cpeer)
+    yg = forward(xg, wg.at[rows_y, cols], ypeer)
+    yu = forward(xu, wu.at[rows_y, cols], ypeer)
     dm = attn_in.shape[1] // 2
 
     def pick(value, flag):
         return jnp.where(flag == 0, value[:, :dm], value[:, dm:])
 
-    for c in local:
-        c.wait()
-    ca.wait_recv()
-    qk = nn(attn_in, wa[:, :768])
-    cos_t = cos_ref[...]
-    sin_t = sin_ref[...]
+    c5.wait_recv()
+    c1.wait_recv()
+    qk = jnp.concatenate([nn(attn_in, w5[0]), nn(attn_in, w1[0])], axis=1)
     qk = (qk * cos_t + swap_halves(qk) * sin_t).astype(BF16)
-    v = nn(attn_in, wa[:, 1280:1536])[:, 64:256].astype(BF16)
+    v = nn(attn_in, w1[1]).astype(BF16)
     kv_own = jnp.concatenate([qk[:, 576:768], v], axis=1)
     kv[0] = kv_own
     kv_copy = remote(kv.at[0], kv.at[1], xpeer)
     a_half[0] = pick(attn_in, s)
     a_half[1] = pick(attn_in, 1 - s)
-    cg = cstep(1, yg)
-    cu = cstep(2, yu)
+    cg = forward(yg, wg.at[rows_c, cols], cpeer)
+    cu = forward(yu, wu.at[rows_c, cols], cpeer)
     kv_copy.wait_recv()
     kv_oth = kv[1]
     groups = H // KV
-    bias = bias_ref[...]
     bias3 = jnp.concatenate([bias] * groups, axis=0)
 
     def stack(value, g):
@@ -546,7 +560,7 @@
         probs[g] = p
         outs.append(nn(p.astype(BF16), vs[g]).astype(BF16))
     attended = jnp.concatenate(unstack(outs), axis=1)
-    w_o = wa[:, 768:1344]
+    w_o = w5[1]
     middle = hidden + nn(attended, w_o)
     rr2 = lax.rsqrt(jnp.mean(middle * middle, axis=-1, keepdims=True) + norm_eps)
     normed2 = middle * rr2
@@ -555,6 +569,8 @@
     t_half[0] = pick(attended, s)
     t_half[1] = pick(attended, 1 - s)
     a_copy = remote(a_half.at[1], a_half.at[2], xpeer)
+    for c in local[6:]:
+        c.wait()
     cot_copy.wait_recv()
     grad_all = jnp.concatenate([cot_ref[...], cot[...]], axis=0)
     d_mix = nt(grad_all, down_ref[...])
@@ -700,9 +716,7 @@
     dv_x[0] = dvb
     dqk_copy = remote(dqk_x.at[0], dqk_x.at[1], xpeer)
     dv_copy = remote(dv_x.at[0], dv_x.at[1], xpeer)
-    da = nt(dqk, wa[:, :768]) + nt(
-        jnp.concatenate([jnp.zeros((rows, 64), BF16), dvb], axis=1), wa[:, 1280:1536]
-    )
+    da = nt(dqk[:, :576], w5[0]) + nt(dqk[:, 576:], w1[0]) + nt(dvb, w1[1])
     gain1 = jnp.sum(da * normed, axis=0, keepdims=True)
     gg_out[...] = jnp.concatenate([gain1, gain2, jnp.zeros((6, gain1.shape[1]), F32)], axis=0)
     gg_copy = remote(gg_out, gg_in, xpeer)
@@ -751,38 +765,57 @@
         c.wait_send()
 
 
+def unpack_kernel(
+    b_ref, i_ref, o1_ref, o2_ref, o3_ref,
+    block_ref, gin_ref, ag_ref, q_ref, k_ref, v_ref, o_ref, fg_ref, gate_ref, up_ref, down_ref,
+):
+    block_ref[...] = b_ref[...]
+    gin_ref[...] = i_ref[...]
+    half = ag_ref.shape[1]
+    ffh = gate_ref.shape[2] // 2
+    for f in range(2):
+        for yy in range(2):
+            for t, ref in enumerate((gate_ref, up_ref)):
+                for zz in range(2):
+                    lo = f * ffh + zz * 384
+                    ref[0, yy * 144 : (yy + 1) * 144, lo : lo + 384] = o1_ref[
+                        f * 8 + yy * 4 + t * 2 + zz
+                    ].astype(F32)
+    down_ref[0] = o2_ref[...].reshape(down_ref.shape[1:]).astype(F32)
+    for r in range(4):
+        lo = r * 80
+        n = 80 if r < 3 else 48
+        rows = slice(lo, lo + n)
+        q_ref[0, rows, :384] = o3_ref[r * 4, :n].astype(F32)
+        mid = o3_ref[r * 4 + 1, :n].astype(F32)
+        q_ref[0, rows, 384:] = mid[:, :192]
+        k_ref[0, rows] = mid[:, 192:]
+        o_ref[0, rows, :384] = o3_ref[r * 4 + 2, :n].astype(F32)
+        last = o3_ref[r * 4 + 3, :n].astype(F32)
+        o_ref[0, rows, 384:] = last[:, :192]
+        v_ref[0, rows] = last[:, 192:]
+    ag_ref[...] = o3_ref[12, 48:64].astype(F32)[0:1, :half]
+    fg_ref[...] = o3_ref[13, 48:64].astype(F32)[0:1, :half]
+
+
 def fused_body(
     tokens, block_order, attn_gain, q_weight, k_weight, v_weight, o_weight, ffn_gain,
     gate_weight, up_weight, down_weight, cotangent,
 ):
     rows, width = tokens.shape
-    s = lax.axis_index("shard")
     half = attn_gain.shape[1]
     ff = gate_weight.shape[2]
-    order = block_order[0]
-    own = lax.dynamic_index_in_dim(order, s, 0, keepdims=False)
-    other = lax.dynamic_index_in_dim(order, 1 - s, 0, keepdims=False)
-    index = jnp.arange(rows, dtype=jnp.int32)
-    q_pos = own * rows + index
-    k_pos = jnp.concatenate([q_pos, other * rows + index])
-    bias = jnp.where(k_pos[None, :] <= q_pos[:, None], 0.0, -1e30).astype(F32)
-    cos_t, sin_t = rope_tables(q_pos, HD)
-    cos_t, sin_t = cos_t[:, 0], sin_t[:, 0]
-    cos_t = jnp.tile(cos_t, (1, 2 * (H + KV)))
-    sin_t = jnp.tile(jnp.concatenate([-sin_t, sin_t], axis=1), (1, H + KV))
-    gains = jnp.concatenate([attn_gain, ffn_gain, jnp.zeros((14, half), BF16)], axis=0)
-    gains = jnp.concatenate(
-        [jnp.where(s == 0, gains, 0), jnp.where(s == 1, gains, 0)], axis=1
-    ).astype(BF16)
-    wa = jnp.concatenate([q_weight[0], k_weight[0], o_weight[0], v_weight[0]], axis=1)
     vm = pl.BlockSpec(memory_space=pltpu.VMEM)
+    hbm = pl.BlockSpec(memory_space=pl.ANY)
     shapes = [(144, 384), (48, width), (80, 384)]
 
     def buf(*shape, dtype=BF16):
         return pltpu.VMEM(shape, dtype)
 
     scratch = [
-        buf(width, 1536), buf(width, ff // 2), buf(width, ff // 2), buf(16, width),
+        buf(rows, width), buf(rows, width), buf(ff // 2, width), buf(2, width, width),
+        buf(2, width, KV * HD), buf(width, ff // 2), buf(width, ff // 2),
+        buf(8, width, dtype=F32), buf(8, width, dtype=F32),
         buf(rows, width), buf(2, rows, 384), buf(2 * rows, width), buf(rows, width),
         buf(rows, width), buf(rows, width), buf(rows, width),
         buf(KV, 3 * rows, 2 * rows, dtype=F32), buf(3, rows, half), buf(3, rows, half),
@@ -793,7 +826,7 @@
         scratch += [buf(count, *sh) for sh in shapes]
     scratch += [
         pltpu.SemaphoreType.DMA((64,)), pltpu.SemaphoreType.DMA((64,)),
-        pltpu.SemaphoreType.DMA((3,)),
+        pltpu.SemaphoreType.DMA((9,)),
     ]
     block_out, input_grad, o1, o2, o3 = pl.pallas_call(
         fused_kernel,
@@ -802,32 +835,30 @@
             jax.ShapeDtypeStruct((rows, width), F32),
             *[jax.ShapeDtypeStruct((16, *sh), BF16) for sh in shapes],
         ),
-        in_specs=[vm] * 10,
+        in_specs=[
+            hbm, pl.BlockSpec(memory_space=pltpu.SMEM), vm, *[hbm] * 4, vm, *[hbm] * 4,
+        ],
         out_specs=[vm] * 5,
         scratch_shapes=scratch,
         compiler_params=pltpu.CompilerParams(
             collective_id=0, has_side_effects=True, vmem_limit_bytes=56 * 1024 * 1024
         ),
     )(
-        tokens, cotangent, cos_t, sin_t, bias, gains, wa, gate_weight[0], up_weight[0],
-        down_weight[0],
-    )
-    gu = o1.reshape(2, 2, 2, 2, 144, 384)
-    gu = gu.transpose(2, 1, 4, 0, 3, 5).reshape(2, half, ff).astype(F32)
-    rest = o3.reshape(4, 4, 80, 384).transpose(0, 2, 1, 3).reshape(320, 1536).astype(F32)
-    return (
-        block_out,
-        input_grad,
-        rest[288:289, :288],
-        rest[None, :288, :576],
-        rest[None, :288, 576:768],
-        rest[None, :288, 1344:],
-        rest[None, :288, 768:1344],
-        rest[288:289, 384 : 384 + 288],
-        gu[0:1],
-        gu[1:2],
-        o2.reshape(1, 768, width).astype(F32),
-    )
+        tokens, block_order, attn_gain, q_weight, k_weight, v_weight, o_weight, ffn_gain,
+        gate_weight, up_weight, down_weight, cotangent,
+    )
+    shapes = [
+        (rows, width), (rows, width), (1, half), (1, half, width), (1, half, KV * HD),
+        (1, half, KV * HD), (1, half, width), (1, half), (1, half, ff), (1, half, ff),
+        (1, ff // 2, width),
+    ]
+    return pl.pallas_call(
+        unpack_kernel,
+        out_shape=tuple(jax.ShapeDtypeStruct(shape, F32) for shape in shapes),
+        in_specs=[vm] * 5,
+        out_specs=(vm,) * 11,
+        compiler_params=pltpu.CompilerParams(vmem_limit_bytes=40 * 1024 * 1024),
+    )(block_out, input_grad, o1, o2, o3)
 
 
 def solution(mesh):

time: 137 us -> 123 us (0.90)
  local copies, waits for them, and re-layouts: 21.9 us -> 14.9 us
  other arithmetic: 3.66 us -> 0 us
  Pallas kernels: 109 us -> 107 us
  between operations: 2.18 us -> 0.67 us
    slice x6 -> x0, local copies, waits for them, and re-layouts: 7.86 us -> none  [the longest x3 3.76 us: fused_body(): gu[1:2]]
    unnamed x33 -> x13, local copies, waits for them, and re-layouts: 6.56 us -> 11.5 us
    pallas_call x1, Pallas kernels: 109 us -> 105 us  [fused_body(): pl.pallas_call(fused_kernel, out_shape=(jax.ShapeDtypeStruct((rows, width...]
    pallas_call x0 -> x3, local copies, waits for them, and re-layouts: none -> 3.42 us  [fused_body(): pl.pallas_call(unpack_kernel, out_shape=tuple((jax.ShapeDtypeStruct(shape...]
    pallas_call x0 -> x1, Pallas kernels: none -> 2.61 us  [fused_body(): pl.pallas_call(unpack_kernel, out_shape=tuple((jax.ShapeDtypeStruct(shape...]
    broadcast_in_dim x3 -> x0, local copies, waits for them, and re-layouts: 2.24 us -> none  [the longest x1 1.2 us: fused_body(): rest[None, :288, 768:1344]]
    convert_element_type x3 -> x0, other arithmetic: 1.98 us -> none  [the longest x1 1.73 us: fused_body(): gu = gu.transpose(2, 1, 4, 0, 3, 5).reshape(2, half, ff).astype(F32)]
    another operation x4 -> x0, local copies, waits for them, and re-layouts: 1.89 us -> none  [the longest x2 0.95 us: fused_body(): cos_t = jnp.tile(cos_t, (1, 2 * (H + KV)))]
where the time goes in v2:
time: 123 us
  Pallas kernels  107 us (87%)
  local copies, waits for them, and re-layouts  14.9 us (12%)
    pallas_call x1, Pallas kernels, fused_body(): pl.pallas_call(fused_kernel, out_shape=(jax.ShapeDtypeStruct((rows, width...  105 us
    unnamed x13, local copies, waits for them, and re-layouts  11.5 us
    pallas_call x3, local copies, waits for them, and re-layouts, fused_body(): pl.pallas_call(unpack_kernel, out_shape=tuple((jax.ShapeDtypeStruct(shape...  3.42 us
    pallas_call x1, Pallas kernels, fused_body(): pl.pallas_call(unpack_kernel, out_shape=tuple((jax.ShapeDtypeStruct(shape...  2.61 us

profile of v2, /device:TPU:25, one launch (start us, length us, event | category | flops | bytes accessed | tf_op | source)
XLA Modules:
  0.0 123.0 jit_solution(14828800723462798141)
XLA Ops:
  0.6 1.7 %copy.23.tok_hbm = bf16[128,576]{1,0:T(8,128)(2,1)} copy(bf16[128,576]{0,1:T(8,128)(2,1)} %param.12) | data formatting | bytes 294912 | tf_op args[0]
  2.4 1.7 %copy.25.cot_hbm = bf16[128,576]{1,0:T(8,128)(2,1)} copy(bf16[128,576]{0,1:T(8,128)(2,1)} %param.23) | data formatting | bytes 294912 | tf_op args[11]
  4.1 2.2 %copy.24.down_hbm = bf16[1,768,576]{2,1,0:T(8,128)(2,1)} copy(bf16[1,768,576]{1,2,0:T(8,128)(2,1)} %param.22) | data formatting | bytes 1769472 | tf_op args[10]
  6.3 104.8 %shard_map.203 = (f32[128,576]{1,0:T(8,128)}, f32[128,576]{1,0:T(8,128)}, bf16[16,144,384]{2,1,0:T(8,128)(2,1)}, bf16[16,48,576]{2,1,0:T(8,128)(2,1)}, bf16[16,80,384]{2,1,0:T(8,128)(2,1)}) custom-call(bf16[128,576]{1,0:T(8,128)(2,1)} %copy.23.tok_hbm, s32[1,2]{1,0:T(1,128)} %order_ref.1, bf16[1,288]{1,0:T(2,128)(2,1)} %again_ref.1, ...), custom_call_target="tpu_custom_call" | custom-call | tf_op jit(solution)/shard_map/pallas_call | solution.py:831
  111.1 0.0 copy-start
  111.1 1.5 %copy-done = bf16[16,144,384]{2,1,0:T(8,128)(2,1)S(1)} copy-done((bf16[16,144,384]{2,1,0:T(8,128)(2,1)S(1)}, bf16[16,144,384]{2,1,0:T(8,128)(2,1)}, u32[]{:S(2)}) %copy-start) | copy-done | bytes 1769496
  112.6 0.0 copy-start.1
  112.6 1.2 copy-done.1
  113.8 0.0 copy-start.2
  113.8 1.2 copy-done.2
  115.0 0.0 copy-start.3
  115.0 1.0 copy-done.3
  116.0 0.0 copy-start.4
  116.0 1.0 copy-done.4
  116.9 2.6 %shard_map.204 = (f32[128,576]{1,0:T(8,128)S(1)}, f32[128,576]{1,0:T(8,128)S(1)}, f32[1,288]{1,0:T(1,128)}, f32[1,288,576]{2,1,0:T(8,128)}, f32[1,288,192]{2,1,0...) custom-call(f32[128,576]{1,0:T(8,128)S(1)} %copy-done.3, ...), custom_call_target="tpu_custom_call" | custom-call | tf_op jit(solution)/shard_map/pallas_call | solution.py:855
  119.5 0.9 copy.26
  120.4 0.9 copy.27
  121.3 1.7 %copy.28 = f32[1,768,576]{1,2,0:T(8,128)} copy(f32[1,768,576]{2,1,0:T(8,128)S(1)} %get-tuple-element.31) | data formatting | bytes 3538944 | tf_op jit(solution)/shard_map/pallas_call | solution.py:855
Async XLA Ops:
  111.1 1.5 %copy-start = (bf16[16,144,384]{2,1,0:T(8,128)(2,1)S(1)}, bf16[16,144,384]{2,1,0:T(8,128)(2,1)}, u32[]{:S(2)}) copy-start(bf16[16,144,384]{2,1,0:T(8,128)(2,1)} %get-tuple-element.18.o1_ref) | copy-start | bytes 5308420
  112.6 1.2 copy-start.1
  113.8 1.2 copy-start.2
  115.0 1.0 copy-start.3
  116.0 1.0 copy-start.4

commit v3 on v2

--- a/solution.py
+++ b/solution.py
@@ -390,11 +390,11 @@
     tok_hbm, order_ref, again_ref, q_hbm, k_hbm, v_hbm, o_hbm, fgain_ref, gate_hbm, up_hbm, down_hbm,
     cot_hbm,
     out_ref, gin_ref, o1_ref, o2_ref, o3_ref,
-    tok_ref, cot_ref, down_ref, w5, w1, wg, wu, gain_ref, gain_in, cot, kv, bb, part_out, part_in, dbo, dbi, probs, a_half, t_half, dm_x,
+    tok_t, cot_t, cot_ref, down_ref, w5, w1, wg, wu, gain_ref, gain_in, cot, kv, bb, part_out, part_in, dbo, dbi, probs, a_half, t_half, dm_x,
     dkv_out, dkv_in, dqk_x, dv_x, gg_out, gg_in, g1, g2, g3, r1a, r1b, r1c, r2a, r2b, r2c,
     r3a, r3b, r3c, f1, f2, f3, send_sem, recv_sem, local_sem,
 ):
-    rows = tok_ref.shape[0]
+    rows = tok_t.shape[1]
     rep = lax.axis_index("rep")
     s = lax.axis_index("shard")
     core = rep % 2
@@ -432,8 +432,8 @@
     pairs = [
         (q_hbm.at[0], w5.at[0, own_rows]), (o_hbm.at[0], w5.at[1, own_rows]),
         (k_hbm.at[0], w1.at[0, own_rows]), (v_hbm.at[0], w1.at[1, own_rows]),
-        (tok_hbm, tok_ref), (cot_hbm, cot_ref), (gate_ref.at[:, ffcols], wg.at[own_rows]),
-        (up_ref.at[:, ffcols], wu.at[own_rows]), (down_hbm.at[0], down_ref),
+        (tok_hbm, tok_t), (cot_hbm, cot_t), (gate_ref.at[:, ffcols], wg.at[own_rows]),
+        (up_ref.at[:, ffcols], wu.at[own_rows]), (down_hbm, down_ref),
     ]
     local = [
         pltpu.make_async_copy(src, dst, local_sem.at[i]) for i, (src, dst) in enumerate(pairs)
@@ -468,6 +468,8 @@
     )
     gain_ref[2:8] = jnp.zeros((6, 2 * half), F32)
 
+    local[5].wait()
+    cot_ref[...] = cot_t[...].astype(F32).T.astype(BF16)
     barrier = pltpu.get_barrier_semaphore()
     for peer in [xpeer, cpeer, ypeer] + zpeers:
         pl.semaphore_signal(barrier, inc=1, device_id=peer, device_id_type=MESH)
@@ -489,7 +491,6 @@
 
     x5 = send(w5.at[core, rows_x], xpeer)
     x1 = send(w1.at[core, rows_x], xpeer)
-    local[5].wait()
     xg = remote(gate_ref.at[part_x, cols_x], wg.at[rows_x, cols], xpeer)
     xu = remote(up_ref.at[part_x, cols_x], wu.at[rows_x, cols], xpeer)
     cot_copy = remote(cot_ref, cot, xpeer)
@@ -502,7 +503,7 @@
     y5 = forward(x5, w5.at[core, rows_y], ypeer)
     y1 = forward(x1, w1.at[core, rows_y], ypeer)
     local[4].wait()
-    hidden = tok_ref[...].astype(F32)
+    hidden = tok_t[...].astype(F32).T
     rr = lax.rsqrt(jnp.mean(hidden * hidden, axis=-1, keepdims=True) + norm_eps)
     normed = hidden * rr
     gain_copy.wait_recv()
@@ -573,7 +574,7 @@
         c.wait()
     cot_copy.wait_recv()
     grad_all = jnp.concatenate([cot_ref[...], cot[...]], axis=0)
-    d_mix = nt(grad_all, down_ref[...])
+    d_mix = nn(grad_all, down_ref[...])
     cg.wait_recv()
     cu.wait_recv()
     b_copy.wait_recv()
@@ -588,7 +589,7 @@
     db = nt(d_gt, wg[...]) + nt(d_up, wu[...])
     dbo[...] = db[rows:].astype(BF16)
     db_copy = remote(dbo, dbi, xpeer)
-    part = nn(mix, down_ref[...])
+    part = nt(mix, down_ref[...])
     part_out[...] = part[rows:].astype(BF16)
     part_copy = remote(part_out, part_in, xpeer)
     t_copy = remote(t_half.at[1], t_half.at[2], xpeer)
@@ -723,6 +724,7 @@
     rs_z(1)
     f = da * attn_g
     gin_ref[...] = dm1 + rr * (f - normed * jnp.mean(f * normed, axis=-1, keepdims=True))
+    slots[0] = ag_z(0)
     for c in (a_copy, t_copy, dm_copy, dqk_copy, dv_copy):
         c.wait_recv()
     a_all = jnp.concatenate([a_half[0], a_half[2]], axis=0)
@@ -748,7 +750,6 @@
             tail = jnp.zeros((32, 384), F32)
         g3[12 + cc, 48:80] = tail.astype(BF16)
     rs_core(2)
-    slots[0] = ag_z(0)
     rs_y(2)
     slots[1] = ag_z(1)
     rs_z(2)
@@ -766,11 +767,21 @@
 
 
 def unpack_kernel(
-    b_ref, i_ref, o1_ref, o2_ref, o3_ref,
+    b_hbm, i_hbm, o1_hbm, o2_hbm, o3_hbm,
     block_ref, gin_ref, ag_ref, q_ref, k_ref, v_ref, o_ref, fg_ref, gate_ref, up_ref, down_ref,
+    b_ref, i_ref, o1_ref, o2_ref, o3_ref, sem,
 ):
-    block_ref[...] = b_ref[...]
-    gin_ref[...] = i_ref[...]
+    pairs = (
+        (b_hbm, b_ref), (i_hbm, i_ref), (o1_hbm, o1_ref), (o2_hbm, o2_ref), (o3_hbm, o3_ref),
+    )
+    copies = [pltpu.make_async_copy(src, dst, sem.at[i]) for i, (src, dst) in enumerate(pairs)]
+    for c in copies:
+        c.start()
+    copies[0].wait()
+    block_ref[...] = b_ref[...].T
+    copies[1].wait()
+    gin_ref[...] = i_ref[...].T
+    copies[2].wait()
     half = ag_ref.shape[1]
     ffh = gate_ref.shape[2] // 2
     for f in range(2):
@@ -781,7 +792,9 @@
                     ref[0, yy * 144 : (yy + 1) * 144, lo : lo + 384] = o1_ref[
                         f * 8 + yy * 4 + t * 2 + zz
                     ].astype(F32)
+    copies[3].wait()
     down_ref[0] = o2_ref[...].reshape(down_ref.shape[1:]).astype(F32)
+    copies[4].wait()
     for r in range(4):
         lo = r * 80
         n = 80 if r < 3 else 48
@@ -813,7 +826,8 @@
         return pltpu.VMEM(shape, dtype)
 
     scratch = [
-        buf(rows, width), buf(rows, width), buf(ff // 2, width), buf(2, width, width),
+        buf(width, rows), buf(width, rows), buf(rows, width), buf(width, ff // 2),
+        buf(2, width, width),
         buf(2, width, KV * HD), buf(width, ff // 2), buf(width, ff // 2),
         buf(8, width, dtype=F32), buf(8, width, dtype=F32),
         buf(rows, width), buf(2, rows, 384), buf(2 * rows, width), buf(rows, width),
@@ -844,21 +858,26 @@
             collective_id=0, has_side_effects=True, vmem_limit_bytes=56 * 1024 * 1024
         ),
     )(
-        tokens, block_order, attn_gain, q_weight, k_weight, v_weight, o_weight, ffn_gain,
-        gate_weight, up_weight, down_weight, cotangent,
-    )
-    shapes = [
-        (rows, width), (rows, width), (1, half), (1, half, width), (1, half, KV * HD),
+        tokens.T, block_order, attn_gain, q_weight, k_weight, v_weight, o_weight, ffn_gain,
+        gate_weight, up_weight, down_weight[0].T, cotangent.T,
+    )
+    out_shapes = [
+        (width, rows), (width, rows), (1, half), (1, half, width), (1, half, KV * HD),
         (1, half, KV * HD), (1, half, width), (1, half), (1, half, ff), (1, half, ff),
         (1, ff // 2, width),
     ]
-    return pl.pallas_call(
+    out = pl.pallas_call(
         unpack_kernel,
-        out_shape=tuple(jax.ShapeDtypeStruct(shape, F32) for shape in shapes),
-        in_specs=[vm] * 5,
+        out_shape=tuple(jax.ShapeDtypeStruct(shape, F32) for shape in out_shapes),
+        in_specs=[hbm] * 5,
         out_specs=(vm,) * 11,
+        scratch_shapes=[
+            buf(rows, width, dtype=F32), buf(rows, width, dtype=F32),
+            *[buf(16, *sh) for sh in shapes], pltpu.SemaphoreType.DMA((5,)),
+        ],
         compiler_params=pltpu.CompilerParams(vmem_limit_bytes=40 * 1024 * 1024),
     )(block_out, input_grad, o1, o2, o3)
+    return (out[0].T, out[1].T, *out[2:])
 
 
 def solution(mesh):

time: 123 us -> 119 us (0.967)
  local copies, waits for them, and re-layouts: 14.9 us -> 7.52 us
  Pallas kernels: 107 us -> 110 us
    unnamed x13 -> x11, local copies, waits for them, and re-layouts: 11.5 us -> 7.52 us
    pallas_call x3 -> x0, local copies, waits for them, and re-layouts: 3.42 us -> none  [fused_body(): pl.pallas_call(unpack_kernel, out_shape=tuple((jax.ShapeDtypeStruct(shape...]
    pallas_call x1, Pallas kernels: 2.61 us -> 4.52 us  [fused_body(): pl.pallas_call(unpack_kernel, out_shape=tuple((jax.ShapeDtypeStruct(shape...]
where the time goes in v3:
time: 119 us
  Pallas kernels  110 us (92%)
  local copies, waits for them, and re-layouts  7.52 us (6%)
    pallas_call x1, Pallas kernels, fused_body(): pl.pallas_call(fused_kernel, out_shape=(jax.ShapeDtypeStruct((rows, width...  106 us
    unnamed x11, local copies, waits for them, and re-layouts  7.52 us
    pallas_call x1, Pallas kernels, fused_body(): pl.pallas_call(unpack_kernel, out_shape=tuple((jax.ShapeDtypeStruct(shape...  4.52 us

profile of v3, /device:TPU:25, one launch (start us, length us, event | category | flops | bytes accessed | tf_op | source)
XLA Modules:
  0.0 118.7 jit_solution(518540400843435919)
XLA Ops:
  0.6 105.9 %shard_map.203 = (f32[128,576]{1,0:T(8,128)}, f32[128,576]{1,0:T(8,128)}, bf16[16,144,384]{2,1,0:T(8,128)(2,1)}, bf16[16,48,576]{2,1,0:T(8,128)(2,1)}, bf16[16,80,384]{2,1,0:T(8,128)(2,1)}) custom-call(bf16[576,128]{1,0:T(8,128)(2,1)} %bitcast.8, s32[1,2]{1,0:T(1,128)} %order_ref.1, bf16[1,288]{1,0:T(2,128)(2,1)} %again_ref.1, bf16[1,288,576]{2,1,0:T(8,128)(2,1)} %q_hbm.1, ...), custom_call_target="tpu_custom_call" | custom-call | tf_op jit(solution)/shard_map/pallas_call | solution.py:845
  106.6 0.0 copy-start
  106.6 1.5 %copy-done = bf16[16,144,384]{2,1,0:T(8,128)(2,1)S(1)} copy-done((bf16[16,144,384]{2,1,0:T(8,128)(2,1)S(1)}, bf16[16,144,384]{2,1,0:T(8,128)(2,1)}, u32[]{:S(2)}) %copy-start) | copy-done | bytes 1769496
  108.1 0.0 copy-start.1
  108.1 1.2 %copy-done.1 = bf16[16,48,576]{2,1,0:T(8,128)(2,1)S(1)} copy-done((bf16[16,48,576]{2,1,0:T(8,128)(2,1)S(1)}, bf16[16,48,576]{2,1,0:T(8,128)(2,1)}, u32[]{:S(2)}) %copy-start.1) | copy-done | bytes 884760
  109.3 0.0 copy-start.2
  109.3 1.2 %copy-done.2 = bf16[16,80,384]{2,1,0:T(8,128)(2,1)S(1)} copy-done((bf16[16,80,384]{2,1,0:T(8,128)(2,1)S(1)}, bf16[16,80,384]{2,1,0:T(8,128)(2,1)}, u32[]{:S(2)}) %copy-start.2) | copy-done | bytes 983064
  110.5 0.0 copy-start.3
  110.5 1.0 copy-done.3
  111.5 0.0 copy-start.4
  111.5 1.0 copy-done.4
  112.4 4.5 %shard_map.204 = (f32[576,128]{1,0:T(8,128)}, f32[576,128]{1,0:T(8,128)}, f32[1,288]{1,0:T(1,128)}, f32[1,288,576]{2,1,0:T(8,128)}, f32[1,288,192]{2,1,0:T(8,128...) custom-call(f32[128,576]{1,0:T(8,128)S(1)} %copy-done.3, ...), custom_call_target="tpu_custom_call" | custom-call | tf_op jit(solution)/shard_map/pallas_call | solution.py:869
  117.0 1.7 %copy.23 = f32[1,768,576]{1,2,0:T(8,128)} copy(f32[1,768,576]{2,1,0:T(8,128)S(1)} %get-tuple-element.53) | data formatting | bytes 3538944
Async XLA Ops:
  106.6 1.5 %copy-start = (bf16[16,144,384]{2,1,0:T(8,128)(2,1)S(1)}, bf16[16,144,384]{2,1,0:T(8,128)(2,1)}, u32[]{:S(2)}) copy-start(bf16[16,144,384]{2,1,0:T(8,128)(2,1)} %get-tuple-element.29.o1_hbm) | copy-start | bytes 5308420
  108.1 1.2 %copy-start.1 = (bf16[16,48,576]{2,1,0:T(8,128)(2,1)S(1)}, bf16[16,48,576]{2,1,0:T(8,128)(2,1)}, u32[]{:S(2)}) copy-start(bf16[16,48,576]{2,1,0:T(8,128)(2,1)} %get-tuple-element.30.o2_hbm) | copy-start | bytes 2654212
  109.3 1.2 %copy-start.2 = (bf16[16,80,384]{2,1,0:T(8,128)(2,1)S(1)}, bf16[16,80,384]{2,1,0:T(8,128)(2,1)}, u32[]{:S(2)}) copy-start(bf16[16,80,384]{2,1,0:T(8,128)(2,1)} %get-tuple-element.31.o3_hbm) | copy-start | bytes 2949124
  110.5 1.0 copy-start.3
  111.5 1.0 copy-start.4

commit v4 on v3

--- a/solution.py
+++ b/solution.py
@@ -708,6 +708,7 @@
     dkv_out[...] = dkv[rows:].astype(BF16)
     dkv_copy = remote(dkv_out, dkv_in, xpeer)
     rs_z(0)
+    rs_z(1)
     dkv_copy.wait_recv()
     dkv = dkv[:rows] + dkv_in[...].astype(F32)
     dqk = jnp.concatenate(unstack(dqs) + [dkv[:, : KV * HD]], axis=1)
@@ -721,7 +722,6 @@
     gain1 = jnp.sum(da * normed, axis=0, keepdims=True)
     gg_out[...] = jnp.concatenate([gain1, gain2, jnp.zeros((6, gain1.shape[1]), F32)], axis=0)
     gg_copy = remote(gg_out, gg_in, xpeer)
-    rs_z(1)
     f = da * attn_g
     gin_ref[...] = dm1 + rr * (f - normed * jnp.mean(f * normed, axis=-1, keepdims=True))
     slots[0] = ag_z(0)
@@ -750,10 +750,10 @@
             tail = jnp.zeros((32, 384), F32)
         g3[12 + cc, 48:80] = tail.astype(BF16)
     rs_core(2)
+    slots[1] = ag_z(1)
     rs_y(2)
-    slots[1] = ag_z(1)
+    ag_y(0)
     rs_z(2)
-    ag_y(0)
     slots[2] = ag_z(2)
     ag_y(1)
     ag_core(0)

time: 119 us -> 119 us (level)
  no operation moved by 1% of the time
where the time goes in v4:
time: 119 us
  Pallas kernels  110 us (92%)
  local copies, waits for them, and re-layouts  7.52 us (6%)
    pallas_call x1, Pallas kernels, fused_body(): pl.pallas_call(fused_kernel, out_shape=(jax.ShapeDtypeStruct((rows, width...  106 us
    unnamed x11, local copies, waits for them, and re-layouts  7.52 us
    pallas_call x1, Pallas kernels, fused_body(): pl.pallas_call(unpack_kernel, out_shape=tuple((jax.ShapeDtypeStruct(shape...  4.52 us

profile of v4, /device:TPU:25, one launch (start us, length us, event | category | flops | bytes accessed | tf_op | source)
XLA Modules:
  0.0 118.7 jit_solution(16305150442973326798)
XLA Ops:
  0.6 106.0 %shard_map.203 = (f32[128,576]{1,0:T(8,128)}, f32[128,576]{1,0:T(8,128)}, bf16[16,144,384]{2,1,0:T(8,128)(2,1)}, bf16[16,48,576]{2,1,0:T(8,128)(2,1)}, bf16[16,80,384]{2,1,0:T(8,128)(2,1)}) custom-call(bf16[576,128]{1,0:T(8,128)(2,1)} %bitcast.8, s32[1,2]{1,0:T(1,128)} %order_ref.1, bf16[1,288]{1,0:T(2,128)(2,1)} %again_ref.1, bf16[1,288,576]{2,1,0:T(8,128)(2,1)} %q_hbm.1, ...), custom_call_target="tpu_custom_call" | custom-call | tf_op jit(solution)/shard_map/pallas_call | solution.py:845
  106.6 0.0 copy-start
  106.6 1.5 %copy-done = bf16[16,144,384]{2,1,0:T(8,128)(2,1)S(1)} copy-done((bf16[16,144,384]{2,1,0:T(8,128)(2,1)S(1)}, bf16[16,144,384]{2,1,0:T(8,128)(2,1)}, u32[]{:S(2)}) %copy-start) | copy-done | bytes 1769496
  108.1 0.0 copy-start.1
  108.1 1.2 %copy-done.1 = bf16[16,48,576]{2,1,0:T(8,128)(2,1)S(1)} copy-done((bf16[16,48,576]{2,1,0:T(8,128)(2,1)S(1)}, bf16[16,48,576]{2,1,0:T(8,128)(2,1)}, u32[]{:S(2)}) %copy-start.1) | copy-done | bytes 884760
  109.3 0.0 copy-start.2
  109.3 1.2 %copy-done.2 = bf16[16,80,384]{2,1,0:T(8,128)(2,1)S(1)} copy-done((bf16[16,80,384]{2,1,0:T(8,128)(2,1)S(1)}, bf16[16,80,384]{2,1,0:T(8,128)(2,1)}, u32[]{:S(2)}) %copy-start.2) | copy-done | bytes 983064
  110.5 0.0 copy-start.3
  110.5 1.0 copy-done.3
  111.5 0.0 copy-start.4
  111.5 1.0 copy-done.4
  112.4 4.5 %shard_map.204 = (f32[576,128]{1,0:T(8,128)}, f32[576,128]{1,0:T(8,128)}, f32[1,288]{1,0:T(1,128)}, f32[1,288,576]{2,1,0:T(8,128)}, f32[1,288,192]{2,1,0:T(8,128...) custom-call(f32[128,576]{1,0:T(8,128)S(1)} %copy-done.3, ...), custom_call_target="tpu_custom_call" | custom-call | tf_op jit(solution)/shard_map/pallas_call | solution.py:869
  117.0 1.7 %copy.23 = f32[1,768,576]{1,2,0:T(8,128)} copy(f32[1,768,576]{2,1,0:T(8,128)S(1)} %get-tuple-element.53) | data formatting | bytes 3538944
Async XLA Ops:
  106.6 1.5 %copy-start = (bf16[16,144,384]{2,1,0:T(8,128)(2,1)S(1)}, bf16[16,144,384]{2,1,0:T(8,128)(2,1)}, u32[]{:S(2)}) copy-start(bf16[16,144,384]{2,1,0:T(8,128)(2,1)} %get-tuple-element.29.o1_hbm) | copy-start | bytes 5308420
  108.1 1.2 %copy-start.1 = (bf16[16,48,576]{2,1,0:T(8,128)(2,1)S(1)}, bf16[16,48,576]{2,1,0:T(8,128)(2,1)}, u32[]{:S(2)}) copy-start(bf16[16,48,576]{2,1,0:T(8,128)(2,1)} %get-tuple-element.30.o2_hbm) | copy-start | bytes 2654212
  109.3 1.2 %copy-start.2 = (bf16[16,80,384]{2,1,0:T(8,128)(2,1)S(1)}, bf16[16,80,384]{2,1,0:T(8,128)(2,1)}, u32[]{:S(2)}) copy-start(bf16[16,80,384]{2,1,0:T(8,128)(2,1)} %get-tuple-element.31.o3_hbm) | copy-start | bytes 2949124
  110.5 1.0 copy-start.3
  111.5 1.0 copy-start.4
